TPU v7x, 32 devices: a whole 2x2x4 slice. The times are simulated.
32 devices in a mesh: row: 16 (over z, x, core), col: 2 (over y).
Axes of the slice: x: 2, y: 2, z: 4, core: 2. Of those that a mesh axis runs over, the one named last changes fastest.
Arguments:
- image: bfloat16 [768, 512, 256], P('row', 'col'), may hold values from -6 to 6
- proj_in: bfloat16 [256, 512], replicated, may hold values from -0.375 to 0.375
- taps_wide: float32 [3, 512], replicated, may hold values from -3 to 3
- taps_tall: float32 [3, 512], replicated, may hold values from -3 to 3
- proj_out: bfloat16 [512, 256], replicated, may hold values from -0.25 to 0.25
- bias: float32 [256], replicated, may hold values from -3 to 3
Outputs:
- result: bfloat16 [768, 512, 256], P('row', 'col')
All inputs are finite; a program needn't handle non-finite values.
Results may differ from a plain program's by a relative error of at most 0.0054.
Values may be sent and summed in bfloat16 or wider, within the bound.
No kernel may reach another device: no remote copies, remote signals or barrier semaphores. Data moves between devices by JAX's collectives and lax.ppermute only.
A program may use at most 192 MiB of HBM per device.

v0:
```python
import jax
import jax.numpy as jnp
from jax import lax
from jax.experimental import pallas as pl
from jax.experimental.pallas import tpu as pltpu
from jax.sharding import PartitionSpec as P

BF16 = jnp.bfloat16
F32 = jnp.float32
MIB = 1 << 20
ROWS = 4


def conv_kernel(before, here, after, top, bot, u_ref, lh_ref, rh_ref, bias_ref, out_ref, shifts):
    i = pl.program_id(0)
    n, w, c = here.shape
    ring = lax.broadcasted_iota(jnp.int32, (w, c), 0)
    first = jnp.where(i == 0, top[0:w, :], before[0])
    last = jnp.where(i == pl.num_programs(0) - 1, bot[0:w, :], after[0])
    rows = [first] + [here[r] for r in range(n)] + [last]
    for r, x in enumerate(rows):
        at = i * n + r
        x32 = x.astype(F32)
        lead, tail = lh_ref[pl.ds(at, 1), :], rh_ref[pl.ds(at, 1), :]
        shifts[r, 0] = jnp.where(ring == 0, lead, pltpu.roll(x32, 1, 0)).astype(BF16)
        shifts[r, 1] = x
        shifts[r, 2] = jnp.where(ring == w - 1, tail, pltpu.roll(x32, w - 1, 0)).astype(BF16)
    lhs = [
        jnp.concatenate([shifts[r + k // 3, k % 3] for k in range(9)], axis=1) for r in range(n)
    ]
    y = jnp.dot(jnp.concatenate(lhs, axis=0), u_ref[...], preferred_element_type=F32)
    bias = bias_ref[...] * 0.5
    for r in range(n):
        half = y[r * w : (r + 1) * w] + bias
        out_ref[r] = (here[r].astype(F32) + (half + half * jnp.tanh(half))).astype(BF16)


def shifted(x, axis, step):
    count = lax.axis_size(axis)
    if step > 0:
        return lax.ppermute(x, axis, [(i, i + 1) for i in range(count - 1)])
    return lax.ppermute(x, axis, [(i + 1, i) for i in range(count - 1)])


def column_halos(image):
    first, last = image[:, 0, :], image[:, -1, :]
    if lax.axis_size("col") == 2:
        low = lax.axis_index("col") == 0
        got = lax.ppermute(jnp.where(low, last, first), "col", [(0, 1), (1, 0)])
        zero = jnp.zeros_like(got)
        return jnp.where(low, zero, got), jnp.where(low, got, zero)
    return shifted(last, "col", 1), shifted(first, "col", -1)


def dense_taps(proj_in, taps_wide, taps_tall, proj_out):
    c = proj_in.shape[0]
    scale = (taps_tall[:, None] * taps_wide[None] * 0.5).reshape(9, 1, -1)
    scaled = (proj_in.astype(F32)[None] * scale).astype(BF16)
    taps = jnp.einsum("kcr,rd->kcd", scaled, proj_out, preferred_element_type=F32)
    return taps.astype(BF16).reshape(9 * c, c)


def on_device(image, proj_in, taps_wide, taps_tall, proj_out, bias):
    th, w, c = image.shape
    lh, rh = column_halos(image)
    u = dense_taps(proj_in, taps_wide, taps_tall, proj_out)

    def extended(at):
        pad = jnp.zeros((14, c), BF16)
        return jnp.concatenate([image[at], lh[at][None], rh[at][None], pad], axis=0)

    top = shifted(extended(-1), "row", 1)
    bot = shifted(extended(0), "row", -1)

    def column(x, at):
        pad = jnp.zeros((6, c), BF16)
        return jnp.concatenate([top[at][None], x, bot[at][None], pad], axis=0).astype(F32)

    def whole(x):
        return pl.BlockSpec(x.shape, lambda i: (0,) * x.ndim)

    small = (top, bot, u, column(lh, w), column(rh, w + 1), bias.reshape(1, c))
    block = pl.BlockSpec((ROWS, w, c), lambda i: (i, 0, 0))
    return pl.pallas_call(
        conv_kernel,
        grid=(th // ROWS,),
        out_shape=jax.ShapeDtypeStruct(image.shape, BF16),
        in_specs=[
            pl.BlockSpec((1, w, c), lambda i: (jnp.maximum(i * ROWS - 1, 0), 0, 0)),
            block,
            pl.BlockSpec((1, w, c), lambda i: (jnp.minimum(i * ROWS + ROWS, th - 1), 0, 0)),
            *[whole(x) for x in small],
        ],
        out_specs=block,
        scratch_shapes=[pltpu.VMEM((ROWS + 2, 3, w, c), BF16)],
        compiler_params=pltpu.CompilerParams(vmem_limit_bytes=48 * MIB),
        name="conv",
    )(image, image, image, *small)


def solution(mesh):
    in_specs = (P("row", "col", None), P(), P(), P(), P(), P())
    out_specs = P("row", "col", None)
    return jax.shard_map(
        on_device, mesh=mesh, in_specs=in_specs, out_specs=out_specs, check_vma=False
    )
```

profile of v0, /device:TPU:16, one launch (start us, length us, event | category | flops | bytes accessed | tf_op | source)
XLA Modules:
  0.0 36.2 jit_solution(15702980295705827430)
XLA Ops:
  0.0 0.0 copy-start
  0.0 0.0 copy-start.1
  0.0 1.1 %fusion.6 = (bf16[48,1,256]{2,1,0:T(2,128)(2,1)S(1)}, bf16[48,1,256]{2,1,0:T(2,128)(2,1)S(1)}) fusion(bf16[48,256,256]{2,1,0:T(8,128)(2,1)} %after.1), kind=kLoop, calls=%fused_computation.17 | loop fusion | bytes 98304 | tf_op jit(solution)/shard_map/slice | solution.py:46
  1.2 1.6 %collective-permute-start = (bf16[48,256]{1,0:T(8,128)(2,1)S(1)}, bf16[48,256]{1,0:T(8,128)(2,1)S(1)}, u32[]{:S(2)}, u32[]{:S(2)}) collective-permute-start(bf16[48,256]{1,0:T(8,128)(2,1)S(1)} %fusion.5), channel_id=1, source_target_pairs={{0,1},{1,0},{2,3},{3,2},{4,5},{5,4},{6,7},{7,6},{8,9},{9,8},{10,11... | collective-permute-start | bytes 73736 | tf_op jit(solution)/shard_map/ppermute | solution.py:49
  2.8 1.0 %slice_bitcast_fusion = (bf16[256,256]{1,0:T(8,128)(2,1)S(1)}, bf16[256,256]{1,0:T(8,128)(2,1)S(1)}) fusion(bf16[48,256,256]{2,1,0:T(8,128)(2,1)} %after.1), kind=kLoop, calls=%fused_computation.8 | loop fusion | bytes 524288 | tf_op jit(solution)/shard_map/squeeze | solution.py:70
  3.8 0.7 %multiply_multiply_fusion = f32[3,3,512]{2,1,0:T(4,128)S(1)} fusion(f32[3,512]{1,0:T(4,128)} %param.8, f32[3,512]{1,0:T(4,128)} %param.9), kind=kLoop, calls=%fused_computation.14 | loop fusion | flops 9216 | bytes 30720 | tf_op jit(solution)/shard_map/mul | solution.py:57
  4.5 0.1 pad.15.clone
  4.6 0.1 pad.7.clone
  4.7 1.0 %convert_element_type.15 = f32[256,512]{1,0:T(8,128)S(1)} convert(bf16[256,512]{1,0:T(8,128)(2,1)} %param.7) | non-fusion elementwise | flops 131072 | bytes 786432 | tf_op jit(solution)/shard_map/convert_element_type | solution.py:58
  5.7 0.0 collective-permute-done
  5.7 0.1 maximum_maximum_fusion.1
  5.8 2.4 %collective-permute-start.2 = (bf16[272,256]{1,0:T(8,128)(2,1)S(1)}, bf16[272,256]{1,0:T(8,128)(2,1)S(1)}, u32[]{:S(2)}, u32[]{:S(2)}) collective-permute-start(bf16[272,256]{1,0:T(8,128)(2,1)S(1)} %get-tuple-element.19), channel_id=1, source_target_pairs={{2,0},{4,2},{6,4},{8,6},{10,8},{12,10},{14,12},{16,14},{18,16},{20... | collective-permute-start | bytes 417800 | tf_op jit(solution)/shard_map/ppermute | solution.py:42
  8.3 0.0 copy-done
  8.3 0.8 %fusion.3 = bf16[9,256,256]{2,1,0:T(8,128)(2,1)S(1)} fusion(f32[9,512]{1,0:T(8,128)S(1)} %mul.50, f32[256,512]{1,0:T(8,128)S(1)} %convert_element_type.15, bf16[512,256]{1,0:T(8,128)(2,1)S(1)} %copy-done), kind=kOutput, calls=%fused_computation.4 | convolution fusion | flops 606928896 | bytes 1984512 | tf_op jit(solution)/shard_map/kcr,rd->kcd/dot_general | solution.py:59
  9.1 1.9 %collective-permute-start.1 = (bf16[272,256]{1,0:T(8,128)(2,1)S(1)}, bf16[272,256]{1,0:T(8,128)(2,1)S(1)}, u32[]{:S(2)}, u32[]{:S(2)}) collective-permute-start(bf16[272,256]{1,0:T(8,128)(2,1)S(1)} %get-tuple-element.20), channel_id=1, source_target_pairs={{0,2},{2,4},{4,6},{6,8},{8,10},{10,12},{12,14},{14,16},{16,18},{18... | collective-permute-start | bytes 417800 | tf_op jit(solution)/shard_map/ppermute | solution.py:41
  11.0 0.0 collective-permute-done.2.bot
  11.0 5.3 %collective-permute-done.1.top = bf16[272,256]{1,0:T(8,128)(2,1)S(1)} collective-permute-done((bf16[272,256]{1,0:T(8,128)(2,1)S(1)}, bf16[272,256]{1,0:T(8,128)(2,1)S(1)}, u32[]{:S(2)}, u32[]{:S(2)}) %collective-permute-start.1) | collective-permute-done | bytes 139296 | tf_op jit(solution)/shard_map/ppermute | solution.py:41
  16.4 0.1 maximum_convert_fusion.1
  16.5 0.0 copy-done.1
  16.5 19.8 %conv.1 = bf16[48,256,256]{2,1,0:T(8,128)(2,1)} custom-call(bf16[48,256,256]{2,1,0:T(8,128)(2,1)} %after.1, bf16[48,256,256]{2,1,0:T(8,128)(2,1)} %after.1, bf16[48,256,256]{2,1,0:T(8,128)(2,1)} %after.1, bf16[272,256]{1,0:T(8,128)(2,1)S(1)} %collective-permute-done.1.top, bf16[272,256]{1,0:T(8,128)(2,1)S(1)} %collective-permute-done.2.bot, ...), custom_call_target="tpu_custom_call" | custom-call | tf_op jit(solution)/shard_map/conv/pallas_call | solution.py:84
  (8 shorter events, 0.1 us)
Async XLA Ops:
  0.0 8.3 %copy-start = (bf16[512,256]{1,0:T(8,128)(2,1)S(1)}, bf16[512,256]{1,0:T(8,128)(2,1)}, u32[]{:S(2)}) copy-start(bf16[512,256]{1,0:T(8,128)(2,1)} %param.10) | copy-start | bytes 786436
  0.0 16.5 %copy-start.1 = (f32[256]{0:T(256)S(1)}, f32[256]{0:T(256)}, u32[]{:S(2)}) copy-start(f32[256]{0:T(256)} %param.11) | copy-start | bytes 3076
  1.2 4.5 %collective-permute-start = (bf16[48,256]{1,0:T(8,128)(2,1)S(1)}, bf16[48,256]{1,0:T(8,128)(2,1)S(1)}, u32[]{:S(2)}, u32[]{:S(2)}) collective-permute-start(bf16[48,256]{1,0:T(8,128)(2,1)S(1)} %fusion.5), channel_id=1, source_target_pairs={{0,1},{1,0},{2,3},{3,2},{4,5},{5,4},{6,7},{7,6},{8,9},{9,8},{10,11... | collective-permute-start | bytes 73736 | tf_op jit(solution)/shard_map/ppermute | solution.py:49
  5.8 5.2 %collective-permute-start.2 = (bf16[272,256]{1,0:T(8,128)(2,1)S(1)}, bf16[272,256]{1,0:T(8,128)(2,1)S(1)}, u32[]{:S(2)}, u32[]{:S(2)}) collective-permute-start(bf16[272,256]{1,0:T(8,128)(2,1)S(1)} %get-tuple-element.19), channel_id=1, source_target_pairs={{2,0},{4,2},{6,4},{8,6},{10,8},{12,10},{14,12},{16,14},{18,16},{20... | collective-permute-start | bytes 417800 | tf_op jit(solution)/shard_map/ppermute | solution.py:42
  9.1 7.3 %collective-permute-start.1 = (bf16[272,256]{1,0:T(8,128)(2,1)S(1)}, bf16[272,256]{1,0:T(8,128)(2,1)S(1)}, u32[]{:S(2)}, u32[]{:S(2)}) collective-permute-start(bf16[272,256]{1,0:T(8,128)(2,1)S(1)} %get-tuple-element.20), channel_id=1, source_target_pairs={{0,2},{2,4},{4,6},{6,8},{8,10},{10,12},{12,14},{14,16},{16,18},{18... | collective-permute-start | bytes 417800 | tf_op jit(solution)/shard_map/ppermute | solution.py:41
where the time goes:
time: 36.5 us; the launch traced here: 36.2 us
  Pallas kernels  19.8 us (54%)
  starting transfers between devices  5.95 us (16%)
  waiting for transfers between devices  5.33 us (15%)
  local copies, waits for them, and re-layouts  2.33 us (6%)
  other arithmetic  1.94 us (5%)
  matrix products  0.79 us (2%)
    pallas_call x1, Pallas kernels, on_device(): pl.pallas_call(conv_kernel, grid=(th // ROWS,), out_shape=jax.ShapeDtypeS...  19.8 us
    ppermute x1, waiting for transfers between devices, shifted(): return lax.ppermute(x, axis, [(i, i + 1) for i in range(count - 1)])  5.32 us
    ppermute x1, starting transfers between devices, shifted(): return lax.ppermute(x, axis, [(i + 1, i) for i in range(count - 1)])  2.44 us
    ppermute x1, starting transfers between devices, shifted(): return lax.ppermute(x, axis, [(i, i + 1) for i in range(count - 1)])  1.92 us
    ppermute x1, starting transfers between devices, column_halos(): got = lax.ppermute(jnp.where(low, last, first), 'col', [(0, 1), (1, 0)])  1.58 us
    slice x1, local copies, waits for them, and re-layouts, column_halos(): first, last = (image[:, 0, :], image[:, -1, :])  1.15 us
    convert_element_type x1, other arithmetic, dense_taps(): scaled = (proj_in.astype(F32)[None] * scale).astype(BF16)  1 us
    squeeze x1, local copies, waits for them, and re-layouts, extended(): return jnp.concatenate([image[at], lh[at][None], rh[at][None], pad], axis=0)  0.98 us
  transfers between devices with their start and end apart: 3, of which 1 were waited for; matrix products, arithmetic and copies ran while one was open for 10% of the time, Pallas kernels for 0%

commit v1 on v0

v1 whole, which is shorter than its diff:
```python
import functools

import jax
import jax.numpy as jnp
from jax import lax
from jax.experimental import pallas as pl
from jax.experimental.pallas import tpu as pltpu
from jax.sharding import PartitionSpec as P

BF16 = jnp.bfloat16
F32 = jnp.float32
MIB = 1 << 20
ROWS = 4


def side_columns(x, lead, tail):
    w = x.shape[0]
    at = lax.broadcasted_iota(jnp.int32, x.shape, 0)
    x32 = x.astype(F32)
    left = jnp.where(at == 0, lead, pltpu.roll(x32, 1, 0))
    right = jnp.where(at == w - 1, tail, pltpu.roll(x32, w - 1, 0))
    return left.astype(BF16), right.astype(BF16)


def convolve(rows, u_ref):
    pairs = range((len(rows) - 2) // 2)

    def term(k, a, b, add):
        parts = []
        for p in pairs:
            sums = [x() + y() if add else x() - y() for x, y in zip(rows[2 * p + a], rows[2 * p + b])]
            parts.append(jnp.concatenate(sums, axis=1))
        lhs = parts[0] if len(parts) == 1 else jnp.concatenate(parts, axis=0)
        return jnp.dot(lhs, u_ref[k], preferred_element_type=F32)

    m1 = term(1, 1, 2, True)
    m2 = term(2, 2, 1, False)
    m0 = term(0, 0, 2, False)
    m3 = term(3, 1, 3, False)
    return m0 + (m1 + m2), (m1 - m2) - m3


def finish(centre, half):
    return (centre.astype(F32) + (half + half * jnp.tanh(half))).astype(BF16)


def store_rows(here, ya, yb, bias_ref, out_ref):
    n, w, _ = here.shape
    bias = bias_ref[...] * 0.5
    for r in range(n):
        y = yb if r % 2 else ya
        part = y[(r // 2) * w : (r // 2 + 1) * w]
        out_ref[r] = finish(here[r], part + bias)


def inner_kernel(before, here, after, u_ref, lh_ref, rh_ref, bias_ref, out_ref, sides):
    i = pl.program_id(0)
    n = here.shape[0]
    base = (i + 1) * n
    centres = [functools.partial(before.__getitem__, 0)]
    centres += [functools.partial(here.__getitem__, r) for r in range(n)]
    centres += [functools.partial(after.__getitem__, 0)]

    def shift(r):
        at = base - 1 + r
        left, right = side_columns(centres[r](), lh_ref[pl.ds(at, 1), :], rh_ref[pl.ds(at, 1), :])
        sides[r, 0] = left
        sides[r, 1] = right

    @pl.when(i == 0)
    def _():
        shift(0)
        shift(1)

    @pl.when(i > 0)
    def _():
        sides[0:2] = sides[n : n + 2]

    for r in range(2, n + 2):
        shift(r)
    rows = [
        (functools.partial(sides.__getitem__, (r, 0)), centres[r],
         functools.partial(sides.__getitem__, (r, 1)))
        for r in range(n + 2)
    ]
    ya, yb = convolve(rows, u_ref)
    store_rows(here, ya, yb, bias_ref, out_ref)


def edge_kernel(here, second, top, bot, u_ref, lh_ref, rh_ref, bias_ref, out_ref, shifts):
    i = pl.program_id(0)
    n, w, _ = here.shape
    height = lh_ref.shape[0] - 8
    rows = [jnp.where(i == 0, top[0:w, :], second[0])]
    rows += [here[r] for r in range(n)]
    rows += [jnp.where(i == 0, second[0], bot[0:w, :])]
    base = i * (height - n)
    for r, x in enumerate(rows):
        lead, tail = lh_ref[pl.ds(base + r, 1), :], rh_ref[pl.ds(base + r, 1), :]
        shifts[r, 0], shifts[r, 2] = side_columns(x, lead, tail)
        shifts[r, 1] = x
    getters = [
        tuple(functools.partial(shifts.__getitem__, (r, k)) for k in range(3)) for r in range(n + 2)
    ]
    ya, yb = convolve(getters, u_ref)
    store_rows(here, ya, yb, bias_ref, out_ref)


def shifted(x, axis, step):
    count = lax.axis_size(axis)
    if step > 0:
        return lax.ppermute(x, axis, [(i, i + 1) for i in range(count - 1)])
    return lax.ppermute(x, axis, [(i + 1, i) for i in range(count - 1)])


def column_halos(image):
    first, last = image[:, 0, :], image[:, -1, :]
    if lax.axis_size("col") == 2:
        low = lax.axis_index("col") == 0
        got = lax.ppermute(jnp.where(low, last, first), "col", [(0, 1), (1, 0)])
        zero = jnp.zeros_like(got)
        return jnp.where(low, zero, got), jnp.where(low, got, zero)
    return shifted(last, "col", 1), shifted(first, "col", -1)


def transformed_taps(proj_in, taps_wide, taps_tall, proj_out):
    c = proj_in.shape[0]
    t0, t1, t2 = taps_tall
    mid = 0.5 * (t0 + t2)
    tall = jnp.stack([t0, mid + 0.5 * t1, mid - 0.5 * t1, t2])
    scale = (tall[:, None] * taps_wide[None] * 0.5).reshape(12, 1, -1)
    scaled = (proj_in.astype(F32)[None] * scale).astype(BF16)
    u = jnp.einsum("kcr,rd->kcd", scaled, proj_out, preferred_element_type=F32)
    return u.astype(BF16).reshape(4, 3 * c, c)


def on_device(image, proj_in, taps_wide, taps_tall, proj_out, bias):
    th, w, c = image.shape
    n = ROWS
    lh, rh = column_halos(image)
    u = transformed_taps(proj_in, taps_wide, taps_tall, proj_out)

    def extended(at):
        pad = jnp.zeros((14, c), BF16)
        return jnp.concatenate([image[at], lh[at][None], rh[at][None], pad], axis=0)

    top = shifted(extended(-1), "row", 1)
    bot = shifted(extended(0), "row", -1)

    def column(x, at):
        pad = jnp.zeros((6, c), BF16)
        return jnp.concatenate([top[at][None], x, bot[at][None], pad], axis=0).astype(F32)

    def whole(x):
        return pl.BlockSpec(x.shape, lambda i: (0,) * x.ndim)

    def one_row(index):
        return pl.BlockSpec((1, w, c), lambda i: (index(i), 0, 0))

    def cost(rows):
        return pl.CostEstimate(
            flops=rows * 12 * w * c * c, bytes_accessed=4 * rows * w * c, transcendentals=rows * w * c)

    params = pltpu.CompilerParams(vmem_limit_bytes=48 * MIB)
    bias2 = bias.reshape(1, c)
    small = (u, lh.astype(F32), rh.astype(F32), bias2)
    inner = pl.pallas_call(
        inner_kernel,
        grid=(th // n - 2,),
        out_shape=jax.ShapeDtypeStruct(image.shape, BF16),
        in_specs=[
            one_row(lambda i: (i + 1) * n - 1),
            pl.BlockSpec((n, w, c), lambda i: (i + 1, 0, 0)),
            one_row(lambda i: (i + 2) * n),
            *[whole(x) for x in small],
        ],
        out_specs=pl.BlockSpec((n, w, c), lambda i: (i + 1, 0, 0)),
        scratch_shapes=[pltpu.VMEM((n + 2, 2, w, c), BF16)],
        compiler_params=params,
        cost_estimate=cost(th - 2 * n),
        name="inner",
    )(image, image, image, *small)

    small = (top, bot, u, column(lh, w), column(rh, w + 1), bias2)
    edges = pl.pallas_call(
        edge_kernel,
        grid=(2,),
        out_shape=jax.ShapeDtypeStruct((2 * n, w, c), BF16),
        in_specs=[
            pl.BlockSpec((n, w, c), lambda i: (i * (th // n - 1), 0, 0)),
            one_row(lambda i: n + i * (th - 2 * n - 1)),
            *[whole(x) for x in small],
        ],
        out_specs=pl.BlockSpec((n, w, c), lambda i: (i, 0, 0)),
        scratch_shapes=[pltpu.VMEM((n + 2, 3, w, c), BF16)],
        compiler_params=params,
        cost_estimate=cost(2 * n),
        name="edges",
    )(image, image, *small)
    out = lax.dynamic_update_slice(inner, edges[:n], (0, 0, 0))
    return lax.dynamic_update_slice(out, edges[n:], (th - n, 0, 0))


def solution(mesh):
    in_specs = (P("row", "col", None), P(), P(), P(), P(), P())
    out_specs = P("row", "col", None)
    return jax.shard_map(
        on_device, mesh=mesh, in_specs=in_specs, out_specs=out_specs, check_vma=False
    )
```

time: 36.5 us -> 34.7 us (0.951)
  the two profiles are of different devices: /device:TPU:16 before, /device:TPU:1 now
where the time goes in v1:
time: 34.7 us; the launch traced here: 34.1 us
  Pallas kernels  18.2 us (52%)
  starting transfers between devices  8.01 us (23%)
  local copies, waits for them, and re-layouts  4 us (12%)
  other arithmetic  2.77 us (8%)
  matrix products  0.99 us (3%)
    pallas_call x1, Pallas kernels, on_device(): pl.pallas_call(inner_kernel, grid=(th // n - 2,), out_shape=jax.ShapeDtyp...  14.6 us
    pallas_call x1, Pallas kernels, on_device(): pl.pallas_call(edge_kernel, grid=(2,), out_shape=jax.ShapeDtypeStruct((2...  3.54 us
    ppermute x1, starting transfers between devices, shifted(): return lax.ppermute(x, axis, [(i, i + 1) for i in range(count - 1)])  3.02 us
    ppermute x1, starting transfers between devices, shifted(): return lax.ppermute(x, axis, [(i + 1, i) for i in range(count - 1)])  2.86 us
    ppermute x1, starting transfers between devices, column_halos(): got = lax.ppermute(jnp.where(low, last, first), 'col', [(0, 1), (1, 0)])  2.13 us
    slice x1, local copies, waits for them, and re-layouts, column_halos(): first, last = (image[:, 0, :], image[:, -1, :])  1.15 us
    convert_element_type x1, other arithmetic, transformed_taps(): scaled = (proj_in.astype(F32)[None] * scale).astype(BF16)  1 us
    dot_general x1, matrix products, transformed_taps(): u = jnp.einsum('kcr,rd->kcd', scaled, proj_out, preferred_element_type=F32)  0.99 us
  transfers between devices with their start and end apart: 3, of which 0 were waited for; matrix products, arithmetic and copies ran while one was open for 14% of the time, Pallas kernels for 43%

profile of v1, /device:TPU:1, one launch (start us, length us, event | category | flops | bytes accessed | tf_op | source)
XLA Modules:
  0.0 34.1 jit_solution(187939341460023950)
XLA Ops:
  0.0 0.0 copy-start
  0.0 0.0 copy-start.1
  0.0 1.1 %fusion.10 = (bf16[48,1,256]{2,1,0:T(2,128)(2,1)S(1)}, bf16[48,1,256]{2,1,0:T(2,128)(2,1)S(1)}) fusion(bf16[48,256,256]{2,1,0:T(8,128)(2,1)} %second.1), kind=kLoop, calls=%fused_computation.26 | loop fusion | bytes 98304 | tf_op jit(solution)/shard_map/slice | solution.py:117
  1.2 2.1 %collective-permute-start = (bf16[48,256]{1,0:T(8,128)(2,1)S(1)}, bf16[48,256]{1,0:T(8,128)(2,1)S(1)}, u32[]{:S(2)}, u32[]{:S(2)}) collective-permute-start(bf16[48,256]{1,0:T(8,128)(2,1)S(1)} %fusion.5), channel_id=1, source_target_pairs={{0,1},{1,0},{2,3},{3,2},{4,5},{5,4},{6,7},{7,6},{8,9},{9,8},{10,11... | collective-permute-start | bytes 73736 | tf_op jit(solution)/shard_map/ppermute | solution.py:120
  3.3 0.8 %fusion.15 = (f32[1,512]{1,0:T(1,128)S(1)}, f32[1,512]{1,0:T(1,128)S(1)}, f32[1,512]{1,0:T(1,128)S(1)}, f32[1,512]{1,0:T(1,128)S(1)}) fusion(f32[3,512]{1,0:T(4,128)} %param.9), kind=kLoop, calls=%fused_computation.31 | loop fusion | flops 2560 | bytes 14336 | tf_op jit(solution)/shard_map/unstack | solution.py:128
  4.2 0.7 %multiply_multiply_fusion = f32[4,3,512]{2,1,0:T(4,128)S(1)} fusion(f32[3,512]{1,0:T(4,128)} %param.8, f32[4,512]{1,0:T(4,128)S(1)} %pad_maximum_fusion), kind=kLoop, calls=%fused_computation.12 | loop fusion | flops 12288 | bytes 38912 | tf_op jit(solution)/shard_map/mul | solution.py:131
  4.9 1.0 %convert_element_type.21 = f32[256,512]{1,0:T(8,128)S(1)} convert(bf16[256,512]{1,0:T(8,128)(2,1)} %param.7) | non-fusion elementwise | flops 131072 | bytes 786432 | tf_op jit(solution)/shard_map/convert_element_type | solution.py:132
  5.9 0.0 copy-done
  5.9 1.0 %fusion.3 = bf16[12,256,256]{2,1,0:T(8,128)(2,1)S(1)} fusion(f32[12,512]{1,0:T(8,128)S(1)} %mul.63, f32[256,512]{1,0:T(8,128)S(1)} %convert_element_type.21, bf16[512,256]{1,0:T(8,128)(2,1)S(1)} %copy-done), kind=kOutput, calls=%fused_computation.4 | convolution fusion | flops 809238528 | bytes 2383872 | tf_op jit(solution)/shard_map/kcr,rd->kcd/dot_general | solution.py:133
  6.9 1.0 %slice_bitcast_fusion = (bf16[256,256]{1,0:T(8,128)(2,1)S(1)}, bf16[256,256]{1,0:T(8,128)(2,1)S(1)}) fusion(bf16[48,256,256]{2,1,0:T(8,128)(2,1)} %second.1), kind=kLoop, calls=%fused_computation.10 | loop fusion | bytes 524288 | tf_op jit(solution)/shard_map/squeeze | solution.py:145
  7.9 0.1 pad.15.clone
  8.0 0.1 pad.7.clone
  8.1 0.0 collective-permute-done
  8.1 0.1 maximum_maximum_fusion.1
  8.2 2.9 %collective-permute-start.2 = (bf16[272,256]{1,0:T(8,128)(2,1)S(1)}, bf16[272,256]{1,0:T(8,128)(2,1)S(1)}, u32[]{:S(2)}, u32[]{:S(2)}) collective-permute-start(bf16[272,256]{1,0:T(8,128)(2,1)S(1)} %get-tuple-element.27), channel_id=1, source_target_pairs={{2,0},{4,2},{6,4},{8,6},{10,8},{12,10},{14,12},{16,14},{18,16},{20... | collective-permute-start | bytes 417800 | tf_op jit(solution)/shard_map/ppermute | solution.py:113
  11.1 3.0 %collective-permute-start.1 = (bf16[272,256]{1,0:T(8,128)(2,1)S(1)}, bf16[272,256]{1,0:T(8,128)(2,1)S(1)}, u32[]{:S(2)}, u32[]{:S(2)}) collective-permute-start(bf16[272,256]{1,0:T(8,128)(2,1)S(1)} %get-tuple-element.28), channel_id=1, source_target_pairs={{0,2},{2,4},{4,6},{6,8},{8,10},{10,12},{12,14},{14,16},{16,18},{18... | collective-permute-start | bytes 417800 | tf_op jit(solution)/shard_map/ppermute | solution.py:112
  14.1 0.0 copy-done.1
  14.1 14.6 %inner.1 = bf16[48,256,256]{2,1,0:T(8,128)(2,1)} custom-call(bf16[48,256,256]{2,1,0:T(8,128)(2,1)} %second.1, bf16[48,256,256]{2,1,0:T(8,128)(2,1)} %second.1, bf16[48,256,256]{2,1,0:T(8,128)(2,1)} %second.1, bf16[4,768,256]{2,1,0:T(8,128)(2,1)S(1)} %bitcast.11, f32[48,256]{1,0:T(8,128)S(1)} %get-tuple-element.21.lh_ref, ...), custom_call_target="tpu_custom_call" | custom-call | flops 8053063680 | bytes 10485760 | tf_op jit(solution)/shard_map/inner/pallas_call | solution.py:167
  28.8 0.0 collective-permute-done.2.bot
  28.8 0.0 collective-permute-done.1.top
  28.8 0.1 maximum_convert_fusion.1
  28.9 3.5 %edges.1 = bf16[8,256,256]{2,1,0:T(8,128)(2,1)S(1)} custom-call(bf16[48,256,256]{2,1,0:T(8,128)(2,1)} %second.1, bf16[48,256,256]{2,1,0:T(8,128)(2,1)} %second.1, bf16[272,256]{1,0:T(8,128)(2,1)S(1)} %collective-permute-done.1.top, bf16[272,256]{1,0:T(8,128)(2,1)S(1)} %collective-permute-done.2.bot, bf16[4,768,256]{2,1,0:T(8,128)(2,1)S(1)} %bitcast.12, ...), custom_call_target="tpu_custom_call" | custom-call | flops 1610612736 | bytes 2097152 | tf_op jit(solution)/shard_map/edges/pallas_call | solution.py:185
  32.4 0.8 %slice_dynamic-update-slice_fusion.1 = bf16[48,256,256]{2,1,0:T(8,128)(2,1)} fusion(bf16[48,256,256]{2,1,0:T(8,128)(2,1)} %inner.1, bf16[8,256,256]{2,1,0:T(8,128)(2,1)S(1)} %edges.1), kind=kLoop, calls=%fused_computation.6 | loop fusion | bytes 1048576 | tf_op jit(solution)/shard_map/dynamic_update_slice | solution.py:200
  33.3 0.8 %slice_dynamic-update-slice_fusion = bf16[48,256,256]{2,1,0:T(8,128)(2,1)} fusion(bf16[48,256,256]{2,1,0:T(8,128)(2,1)} %slice_dynamic-update-slice_fusion.1, bf16[8,256,256]{2,1,0:T(8,128)(2,1)S(1)} %edges.1), kind=kLoop, calls=%fused_computation.5 | loop fusion | bytes 1048576 | tf_op jit(solution)/shard_map/dynamic_update_slice | solution.py:201
  (9 shorter events, 0.1 us)
Async XLA Ops:
  0.0 5.9 %copy-start = (bf16[512,256]{1,0:T(8,128)(2,1)S(1)}, bf16[512,256]{1,0:T(8,128)(2,1)}, u32[]{:S(2)}) copy-start(bf16[512,256]{1,0:T(8,128)(2,1)} %param.10) | copy-start | bytes 786436
  0.0 14.1 %copy-start.1 = (f32[256]{0:T(256)S(1)}, f32[256]{0:T(256)}, u32[]{:S(2)}) copy-start(f32[256]{0:T(256)} %param.11) | copy-start | bytes 3076
  1.2 6.9 %collective-permute-start = (bf16[48,256]{1,0:T(8,128)(2,1)S(1)}, bf16[48,256]{1,0:T(8,128)(2,1)S(1)}, u32[]{:S(2)}, u32[]{:S(2)}) collective-permute-start(bf16[48,256]{1,0:T(8,128)(2,1)S(1)} %fusion.5), channel_id=1, source_target_pairs={{0,1},{1,0},{2,3},{3,2},{4,5},{5,4},{6,7},{7,6},{8,9},{9,8},{10,11... | collective-permute-start | bytes 73736 | tf_op jit(solution)/shard_map/ppermute | solution.py:120
  8.2 20.5 %collective-permute-start.2 = (bf16[272,256]{1,0:T(8,128)(2,1)S(1)}, bf16[272,256]{1,0:T(8,128)(2,1)S(1)}, u32[]{:S(2)}, u32[]{:S(2)}) collective-permute-start(bf16[272,256]{1,0:T(8,128)(2,1)S(1)} %get-tuple-element.27), channel_id=1, source_target_pairs={{2,0},{4,2},{6,4},{8,6},{10,8},{12,10},{14,12},{16,14},{18,16},{20... | collective-permute-start | bytes 417800 | tf_op jit(solution)/shard_map/ppermute | solution.py:113
  11.1 17.7 %collective-permute-start.1 = (bf16[272,256]{1,0:T(8,128)(2,1)S(1)}, bf16[272,256]{1,0:T(8,128)(2,1)S(1)}, u32[]{:S(2)}, u32[]{:S(2)}) collective-permute-start(bf16[272,256]{1,0:T(8,128)(2,1)S(1)} %get-tuple-element.28), channel_id=1, source_target_pairs={{0,2},{2,4},{4,6},{6,8},{8,10},{10,12},{12,14},{14,16},{16,18},{18... | collective-permute-start | bytes 417800 | tf_op jit(solution)/shard_map/ppermute | solution.py:112

commit v2 on v0

v2 whole, which is shorter than its diff:
```python
import jax
import jax.numpy as jnp
from jax import lax
from jax.experimental import pallas as pl
from jax.experimental.pallas import tpu as pltpu
from jax.sharding import PartitionSpec as P

BF16 = jnp.bfloat16
F32 = jnp.float32
MIB = 1 << 20
ROWS = 8


def side_columns(x, lead, tail):
    w = x.shape[0]
    at = lax.broadcasted_iota(jnp.int32, x.shape, 0)
    x32 = x.astype(F32)
    left = jnp.where(at == 0, lead, pltpu.roll(x32, 1, 0))
    right = jnp.where(at == w - 1, tail, pltpu.roll(x32, w - 1, 0))
    return left.astype(BF16), right.astype(BF16)


def conv_kernel(before, here, after, top, bot, u_ref, lh_ref, rh_ref, bias_ref, out_ref,
                ends, sides):
    i = pl.program_id(0)
    n, w, _ = here.shape
    bias = bias_ref[...] * 0.5

    def centre(r):
        return here[r - 1] if 0 < r <= n else ends[r // n]

    def shift(r):
        at = i * n + r
        lead, tail = lh_ref[pl.ds(at, 1), :], rh_ref[pl.ds(at, 1), :]
        sides[r, 0], sides[r, 1] = side_columns(centre(r), lead, tail)

    def row(r):
        return sides[r, 0], centre(r), sides[r, 1]

    def product(k, a, b, add):
        sums = [x + y if add else x - y for x, y in zip(row(a), row(b))]
        return jnp.dot(jnp.concatenate(sums, axis=1), u_ref[k], preferred_element_type=F32)

    def finish(r, half):
        x = here[r].astype(F32)
        out_ref[r] = (x + (half + half * jnp.tanh(half))).astype(BF16)

    ends[0] = jnp.where(i == 0, top[0:w, :], before[0])
    ends[1] = jnp.where(i == pl.num_programs(0) - 1, bot[0:w, :], after[0])
    shift(0)
    shift(1)
    for r in range(0, n, 2):
        shift(r + 2)
        shift(r + 3)
        m1 = product(1, r + 1, r + 2, True)
        m2 = product(2, r + 2, r + 1, False)
        m0 = product(0, r, r + 2, False)
        m3 = product(3, r + 1, r + 3, False)
        finish(r, m0 + (m1 + m2) + bias)
        finish(r + 1, (m1 - m2) - m3 + bias)


def shifted(x, axis, step):
    count = lax.axis_size(axis)
    if step > 0:
        return lax.ppermute(x, axis, [(i, i + 1) for i in range(count - 1)])
    return lax.ppermute(x, axis, [(i + 1, i) for i in range(count - 1)])


def column_halos(image):
    first, last = image[:, 0, :], image[:, -1, :]
    if lax.axis_size("col") == 2:
        low = lax.axis_index("col") == 0
        got = lax.ppermute(jnp.where(low, last, first), "col", [(0, 1), (1, 0)])
        zero = jnp.zeros_like(got)
        return jnp.where(low, zero, got), jnp.where(low, got, zero)
    return shifted(last, "col", 1), shifted(first, "col", -1)


def transformed_taps(proj_in, taps_wide, taps_tall, proj_out):
    c = proj_in.shape[0]
    t0, t1, t2 = taps_tall
    mid = 0.5 * (t0 + t2)
    tall = jnp.stack([t0, mid + 0.5 * t1, mid - 0.5 * t1, t2])
    scale = (tall[:, None] * taps_wide[None] * 0.5).reshape(12, 1, -1)
    scaled = (proj_in.astype(F32)[None] * scale).astype(BF16)
    u = jnp.einsum("kcr,rd->kcd", scaled, proj_out, preferred_element_type=F32)
    return u.astype(BF16).reshape(4, 3 * c, c)


def on_device(image, proj_in, taps_wide, taps_tall, proj_out, bias):
    th, w, c = image.shape
    n = ROWS
    lh, rh = column_halos(image)
    u = transformed_taps(proj_in, taps_wide, taps_tall, proj_out)

    def extended(at):
        pad = jnp.zeros((14, c), BF16)
        return jnp.concatenate([image[at], lh[at][None], rh[at][None], pad], axis=0)

    top = shifted(extended(-1), "row", 1)
    bot = shifted(extended(0), "row", -1)

    def column(x, at):
        pad = jnp.zeros((6, c), BF16)
        return jnp.concatenate([top[at][None], x, bot[at][None], pad], axis=0).astype(F32)

    def whole(x):
        return pl.BlockSpec(x.shape, lambda i: (0,) * x.ndim)

    def one_row(index):
        return pl.BlockSpec((1, w, c), lambda i: (index(i), 0, 0))

    small = (top, bot, u, column(lh, w), column(rh, w + 1), bias.reshape(1, c))
    block = pl.BlockSpec((n, w, c), lambda i: (i, 0, 0))
    return pl.pallas_call(
        conv_kernel,
        grid=(th // n,),
        out_shape=jax.ShapeDtypeStruct(image.shape, BF16),
        in_specs=[
            one_row(lambda i: jnp.maximum(i * n - 1, 0)),
            block,
            one_row(lambda i: jnp.minimum(i * n + n, th - 1)),
            *[whole(x) for x in small],
        ],
        out_specs=block,
        scratch_shapes=[pltpu.VMEM((2, w, c), BF16), pltpu.VMEM((n + 2, 2, w, c), BF16)],
        compiler_params=pltpu.CompilerParams(vmem_limit_bytes=48 * MIB),
        name="conv",
    )(image, image, image, *small)


def solution(mesh):
    in_specs = (P("row", "col", None), P(), P(), P(), P(), P())
    out_specs = P("row", "col", None)
    return jax.shard_map(
        on_device, mesh=mesh, in_specs=in_specs, out_specs=out_specs, check_vma=False
    )
```

time: 36.5 us -> 34.7 us (0.951)
  the two profiles are of different devices: /device:TPU:16 before, /device:TPU:24 now
where the time goes in v2:
time: 34.7 us; the launch traced here: 34.3 us
  Pallas kernels  16.9 us (49%)
  starting transfers between devices  5.94 us (17%)
  waiting for transfers between devices  5.33 us (15%)
  other arithmetic  2.76 us (8%)
  local copies, waits for them, and re-layouts  2.34 us (7%)
  matrix products  0.99 us (3%)
    pallas_call x1, Pallas kernels, on_device(): pl.pallas_call(conv_kernel, grid=(th // n,), out_shape=jax.ShapeDtypeStru...  16.9 us
    ppermute x1, waiting for transfers between devices, shifted(): return lax.ppermute(x, axis, [(i, i + 1) for i in range(count - 1)])  5.32 us
    ppermute x1, starting transfers between devices, shifted(): return lax.ppermute(x, axis, [(i + 1, i) for i in range(count - 1)])  2.44 us
    ppermute x1, starting transfers between devices, shifted(): return lax.ppermute(x, axis, [(i, i + 1) for i in range(count - 1)])  1.91 us
    ppermute x1, starting transfers between devices, column_halos(): got = lax.ppermute(jnp.where(low, last, first), 'col', [(0, 1), (1, 0)])  1.58 us
    slice x1, local copies, waits for them, and re-layouts, column_halos(): first, last = (image[:, 0, :], image[:, -1, :])  1.15 us
    convert_element_type x1, other arithmetic, transformed_taps(): scaled = (proj_in.astype(F32)[None] * scale).astype(BF16)  1 us
    dot_general x1, matrix products, transformed_taps(): u = jnp.einsum('kcr,rd->kcd', scaled, proj_out, preferred_element_type=F32)  0.99 us
  transfers between devices with their start and end apart: 3, of which 1 were waited for; matrix products, arithmetic and copies ran while one was open for 14% of the time, Pallas kernels for 0%

profile of v2, /device:TPU:24, one launch (start us, length us, event | category | flops | bytes accessed | tf_op | source)
XLA Modules:
  0.0 34.3 jit_solution(12537940890281782518)
XLA Ops:
  0.0 0.0 copy-start
  0.0 0.0 copy-start.1
  0.0 1.1 %fusion.8 = (bf16[48,1,256]{2,1,0:T(2,128)(2,1)S(1)}, bf16[48,1,256]{2,1,0:T(2,128)(2,1)S(1)}) fusion(bf16[48,256,256]{2,1,0:T(8,128)(2,1)} %after.1), kind=kLoop, calls=%fused_computation.22 | loop fusion | bytes 98304 | tf_op jit(solution)/shard_map/slice | solution.py:71
  1.2 1.6 %collective-permute-start = (bf16[48,256]{1,0:T(8,128)(2,1)S(1)}, bf16[48,256]{1,0:T(8,128)(2,1)S(1)}, u32[]{:S(2)}, u32[]{:S(2)}) collective-permute-start(bf16[48,256]{1,0:T(8,128)(2,1)S(1)} %fusion.5), channel_id=1, source_target_pairs={{0,1},{1,0},{2,3},{3,2},{4,5},{5,4},{6,7},{7,6},{8,9},{9,8},{10,11... | collective-permute-start | bytes 73736 | tf_op jit(solution)/shard_map/ppermute | solution.py:74
  2.8 1.0 %slice_bitcast_fusion = (bf16[256,256]{1,0:T(8,128)(2,1)S(1)}, bf16[256,256]{1,0:T(8,128)(2,1)S(1)}) fusion(bf16[48,256,256]{2,1,0:T(8,128)(2,1)} %after.1), kind=kLoop, calls=%fused_computation.8 | loop fusion | bytes 524288 | tf_op jit(solution)/shard_map/squeeze | solution.py:99
  3.8 0.8 %fusion.13 = (f32[1,512]{1,0:T(1,128)S(1)}, f32[1,512]{1,0:T(1,128)S(1)}, f32[1,512]{1,0:T(1,128)S(1)}, f32[1,512]{1,0:T(1,128)S(1)}) fusion(f32[3,512]{1,0:T(4,128)} %param.9), kind=kLoop, calls=%fused_computation.27 | loop fusion | flops 2560 | bytes 14336 | tf_op jit(solution)/shard_map/unstack | solution.py:82
  4.6 0.7 %multiply_multiply_fusion = f32[4,3,512]{2,1,0:T(4,128)S(1)} fusion(f32[3,512]{1,0:T(4,128)} %param.8, f32[4,512]{1,0:T(4,128)S(1)} %pad_maximum_fusion), kind=kLoop, calls=%fused_computation.10 | loop fusion | flops 12288 | bytes 38912 | tf_op jit(solution)/shard_map/mul | solution.py:85
  5.3 1.0 %convert_element_type.15 = f32[256,512]{1,0:T(8,128)S(1)} convert(bf16[256,512]{1,0:T(8,128)(2,1)} %param.7) | non-fusion elementwise | flops 131072 | bytes 786432 | tf_op jit(solution)/shard_map/convert_element_type | solution.py:86
  6.4 0.1 pad.19.clone
  6.4 0.0 collective-permute-done
  6.5 0.1 maximum_maximum_fusion.1
  6.6 2.4 %collective-permute-start.2 = (bf16[272,256]{1,0:T(8,128)(2,1)S(1)}, bf16[272,256]{1,0:T(8,128)(2,1)S(1)}, u32[]{:S(2)}, u32[]{:S(2)}) collective-permute-start(bf16[272,256]{1,0:T(8,128)(2,1)S(1)} %get-tuple-element.23), channel_id=1, source_target_pairs={{2,0},{4,2},{6,4},{8,6},{10,8},{12,10},{14,12},{16,14},{18,16},{20... | collective-permute-start | bytes 417800 | tf_op jit(solution)/shard_map/ppermute | solution.py:67
  9.0 0.0 copy-done
  9.0 1.0 %fusion.3 = bf16[12,256,256]{2,1,0:T(8,128)(2,1)S(1)} fusion(f32[12,512]{1,0:T(8,128)S(1)} %mul.63, f32[256,512]{1,0:T(8,128)S(1)} %convert_element_type.15, bf16[512,256]{1,0:T(8,128)(2,1)S(1)} %copy-done), kind=kOutput, calls=%fused_computation.4 | convolution fusion | flops 809238528 | bytes 2383872 | tf_op jit(solution)/shard_map/kcr,rd->kcd/dot_general | solution.py:87
  10.1 0.1 pad.7.clone
  10.1 1.9 %collective-permute-start.1 = (bf16[272,256]{1,0:T(8,128)(2,1)S(1)}, bf16[272,256]{1,0:T(8,128)(2,1)S(1)}, u32[]{:S(2)}, u32[]{:S(2)}) collective-permute-start(bf16[272,256]{1,0:T(8,128)(2,1)S(1)} %get-tuple-element.24), channel_id=1, source_target_pairs={{0,2},{2,4},{4,6},{6,8},{8,10},{10,12},{12,14},{14,16},{16,18},{18... | collective-permute-start | bytes 417800 | tf_op jit(solution)/shard_map/ppermute | solution.py:66
  12.0 0.0 collective-permute-done.2.bot
  12.1 5.3 %collective-permute-done.1.top = bf16[272,256]{1,0:T(8,128)(2,1)S(1)} collective-permute-done((bf16[272,256]{1,0:T(8,128)(2,1)S(1)}, bf16[272,256]{1,0:T(8,128)(2,1)S(1)}, u32[]{:S(2)}, u32[]{:S(2)}) %collective-permute-start.1) | collective-permute-done | bytes 139296 | tf_op jit(solution)/shard_map/ppermute | solution.py:66
  17.4 0.1 maximum_convert_fusion.1
  17.5 0.0 copy-done.1
  17.5 16.9 %conv.1 = bf16[48,256,256]{2,1,0:T(8,128)(2,1)} custom-call(bf16[48,256,256]{2,1,0:T(8,128)(2,1)} %after.1, bf16[48,256,256]{2,1,0:T(8,128)(2,1)} %after.1, bf16[48,256,256]{2,1,0:T(8,128)(2,1)} %after.1, bf16[272,256]{1,0:T(8,128)(2,1)S(1)} %collective-permute-done.1.top, bf16[272,256]{1,0:T(8,128)(2,1)S(1)} %collective-permute-done.2.bot, ...), custom_call_target="tpu_custom_call" | custom-call | tf_op jit(solution)/shard_map/conv/pallas_call | solution.py:116
  (9 shorter events, 0.1 us)
Async XLA Ops:
  0.0 9.0 %copy-start = (bf16[512,256]{1,0:T(8,128)(2,1)S(1)}, bf16[512,256]{1,0:T(8,128)(2,1)}, u32[]{:S(2)}) copy-start(bf16[512,256]{1,0:T(8,128)(2,1)} %param.10) | copy-start | bytes 786436
  0.0 17.5 %copy-start.1 = (f32[256]{0:T(256)S(1)}, f32[256]{0:T(256)}, u32[]{:S(2)}) copy-start(f32[256]{0:T(256)} %param.11) | copy-start | bytes 3076
  1.2 5.3 %collective-permute-start = (bf16[48,256]{1,0:T(8,128)(2,1)S(1)}, bf16[48,256]{1,0:T(8,128)(2,1)S(1)}, u32[]{:S(2)}, u32[]{:S(2)}) collective-permute-start(bf16[48,256]{1,0:T(8,128)(2,1)S(1)} %fusion.5), channel_id=1, source_target_pairs={{0,1},{1,0},{2,3},{3,2},{4,5},{5,4},{6,7},{7,6},{8,9},{9,8},{10,11... | collective-permute-start | bytes 73736 | tf_op jit(solution)/shard_map/ppermute | solution.py:74
  6.6 5.5 %collective-permute-start.2 = (bf16[272,256]{1,0:T(8,128)(2,1)S(1)}, bf16[272,256]{1,0:T(8,128)(2,1)S(1)}, u32[]{:S(2)}, u32[]{:S(2)}) collective-permute-start(bf16[272,256]{1,0:T(8,128)(2,1)S(1)} %get-tuple-element.23), channel_id=1, source_target_pairs={{2,0},{4,2},{6,4},{8,6},{10,8},{12,10},{14,12},{16,14},{18,16},{20... | collective-permute-start | bytes 417800 | tf_op jit(solution)/shard_map/ppermute | solution.py:67
  10.1 7.3 %collective-permute-start.1 = (bf16[272,256]{1,0:T(8,128)(2,1)S(1)}, bf16[272,256]{1,0:T(8,128)(2,1)S(1)}, u32[]{:S(2)}, u32[]{:S(2)}) collective-permute-start(bf16[272,256]{1,0:T(8,128)(2,1)S(1)} %get-tuple-element.24), channel_id=1, source_target_pairs={{0,2},{2,4},{4,6},{6,8},{8,10},{10,12},{12,14},{14,16},{16,18},{18... | collective-permute-start | bytes 417800 | tf_op jit(solution)/shard_map/ppermute | solution.py:66

commit v3 on v2

--- a/solution.py
+++ b/solution.py
@@ -45,8 +45,8 @@
         x = here[r].astype(F32)
         out_ref[r] = (x + (half + half * jnp.tanh(half))).astype(BF16)
 
-    ends[0] = jnp.where(i == 0, top[0:w, :], before[0])
-    ends[1] = jnp.where(i == pl.num_programs(0) - 1, bot[0:w, :], after[0])
+    ends[0] = jnp.where(i == 0, top[...], before[0])
+    ends[1] = jnp.where(i == pl.num_programs(0) - 1, bot[...], after[0])
     shift(0)
     shift(1)
     for r in range(0, n, 2):
@@ -60,6 +60,28 @@
         finish(r + 1, (m1 - m2) - m3 + bias)
 
 
+def ends_kernel(first, last, left, right, rows_ref, cols_ref):
+    rows_ref[0] = first[0]
+    rows_ref[1] = last[0]
+    for r in range(left.shape[0]):
+        cols_ref[0, r : r + 1, :] = left[r].astype(F32)[:1]
+        cols_ref[1, r : r + 1, :] = right[r].astype(F32)[-1:]
+
+
+def weights_kernel(pin_ref, tw_ref, tt_ref, po_ref, u_ref, scaled):
+    pin = pin_ref[...].astype(F32)
+    c = pin.shape[0]
+    t0, t1, t2 = tt_ref[0:1, :], tt_ref[1:2, :], tt_ref[2:3, :]
+    mid = 0.5 * (t0 + t2)
+    for k, tall in enumerate((t0, mid + 0.5 * t1, mid - 0.5 * t1, t2)):
+        for j in range(3):
+            scaled[3 * k + j] = (pin * (tall * tw_ref[j : j + 1, :] * 0.5)).astype(BF16)
+    for k in range(4):
+        for j in range(3):
+            u = jnp.dot(scaled[3 * k + j], po_ref[...], preferred_element_type=F32)
+            u_ref[k, j * c : (j + 1) * c, :] = u.astype(BF16)
+
+
 def shifted(x, axis, step):
     count = lax.axis_size(axis)
     if step > 0:
@@ -67,8 +89,22 @@
     return lax.ppermute(x, axis, [(i + 1, i) for i in range(count - 1)])
 
 
-def column_halos(image):
-    first, last = image[:, 0, :], image[:, -1, :]
+def row_halos(first, last):
+    count = lax.axis_size("row")
+    if count % 2:
+        return shifted(last, "row", 1), shifted(first, "row", -1)
+    even = lax.axis_index("row") % 2 == 0
+
+    def swap(x, start):
+        pairs = [(i, i + 1) for i in range(start, count - 1, 2)]
+        return lax.ppermute(x, "row", pairs + [(b, a) for a, b in pairs])
+
+    got = swap(jnp.where(even, last, first), 0)
+    far = swap(jnp.where(even, first, last), 1)
+    return jnp.where(even, far, got), jnp.where(even, got, far)
+
+
+def column_halos(first, last):
     if lax.axis_size("col") == 2:
         low = lax.axis_index("col") == 0
         got = lax.ppermute(jnp.where(low, last, first), "col", [(0, 1), (1, 0)])
@@ -77,41 +113,55 @@
     return shifted(last, "col", 1), shifted(first, "col", -1)
 
 
-def transformed_taps(proj_in, taps_wide, taps_tall, proj_out):
-    c = proj_in.shape[0]
-    t0, t1, t2 = taps_tall
-    mid = 0.5 * (t0 + t2)
-    tall = jnp.stack([t0, mid + 0.5 * t1, mid - 0.5 * t1, t2])
-    scale = (tall[:, None] * taps_wide[None] * 0.5).reshape(12, 1, -1)
-    scaled = (proj_in.astype(F32)[None] * scale).astype(BF16)
-    u = jnp.einsum("kcr,rd->kcd", scaled, proj_out, preferred_element_type=F32)
-    return u.astype(BF16).reshape(4, 3 * c, c)
-
-
 def on_device(image, proj_in, taps_wide, taps_tall, proj_out, bias):
     th, w, c = image.shape
     n = ROWS
-    lh, rh = column_halos(image)
-    u = transformed_taps(proj_in, taps_wide, taps_tall, proj_out)
-
-    def extended(at):
-        pad = jnp.zeros((14, c), BF16)
-        return jnp.concatenate([image[at], lh[at][None], rh[at][None], pad], axis=0)
-
-    top = shifted(extended(-1), "row", 1)
-    bot = shifted(extended(0), "row", -1)
-
-    def column(x, at):
-        pad = jnp.zeros((6, c), BF16)
-        return jnp.concatenate([top[at][None], x, bot[at][None], pad], axis=0).astype(F32)
 
     def whole(x):
-        return pl.BlockSpec(x.shape, lambda i: (0,) * x.ndim)
+        return pl.BlockSpec(x.shape, lambda i: (0,) * len(x.shape))
 
     def one_row(index):
         return pl.BlockSpec((1, w, c), lambda i: (index(i), 0, 0))
 
-    small = (top, bot, u, column(lh, w), column(rh, w + 1), bias.reshape(1, c))
+    def some_columns(at):
+        return pl.BlockSpec((th, 16, c), lambda i: (0, at, 0))
+
+    params = pltpu.CompilerParams(vmem_limit_bytes=48 * MIB)
+    ends = jax.ShapeDtypeStruct((2, w, c), BF16), jax.ShapeDtypeStruct((2, th, c), F32)
+    rows, cols = pl.pallas_call(
+        ends_kernel,
+        grid=(1,),
+        out_shape=ends,
+        in_specs=[one_row(lambda i: 0), one_row(lambda i: th - 1),
+                  some_columns(0), some_columns(w // 16 - 1)],
+        out_specs=tuple(whole(x) for x in ends),
+        compiler_params=params,
+        name="ends",
+    )(image, image, image, image)
+    top, bot = row_halos(rows[0], rows[1])
+
+    args = (proj_in, taps_wide, taps_tall, proj_out)
+    weights = jax.ShapeDtypeStruct((4, 3 * c, c), BF16)
+    u = pl.pallas_call(
+        weights_kernel,
+        grid=(1,),
+        out_shape=weights,
+        in_specs=[whole(x) for x in args],
+        out_specs=whole(weights),
+        scratch_shapes=[pltpu.VMEM((12,) + proj_in.shape, BF16)],
+        compiler_params=params,
+        cost_estimate=pl.CostEstimate(
+            flops=24 * c * c * proj_in.shape[1], bytes_accessed=3 * MIB, transcendentals=0),
+        name="weights",
+    )(*args)
+
+    def column(k, at):
+        pad = jnp.zeros((14, c), BF16)
+        return jnp.concatenate(
+            [top[at][None], cols[k].astype(BF16), bot[at][None], pad], axis=0)
+
+    lh, rh = column_halos(column(0, 0), column(1, w - 1))
+    small = (top, bot, u, lh.astype(F32), rh.astype(F32), bias.reshape(1, c))
     block = pl.BlockSpec((n, w, c), lambda i: (i, 0, 0))
     return pl.pallas_call(
         conv_kernel,
@@ -125,7 +175,7 @@
         ],
         out_specs=block,
         scratch_shapes=[pltpu.VMEM((2, w, c), BF16), pltpu.VMEM((n + 2, 2, w, c), BF16)],
-        compiler_params=pltpu.CompilerParams(vmem_limit_bytes=48 * MIB),
+        compiler_params=params,
         name="conv",
     )(image, image, image, *small)
 

time: 34.7 us -> 30.4 us (0.88)
  the two profiles are of different devices: /device:TPU:24 before, /device:TPU:25 now
where the time goes in v3:
time: 30.4 us; the launch traced here: 30.2 us
  Pallas kernels  19.2 us (63%)
  waiting for transfers between devices  5.6 us (18%)
  starting transfers between devices  5.06 us (17%)
    pallas_call x1, Pallas kernels, on_device(): pl.pallas_call(conv_kernel, grid=(th // n,), out_shape=jax.ShapeDtypeStru...  16.8 us
    ppermute x2, waiting for transfers between devices, swap(): return lax.ppermute(x, 'row', pairs + [(b, a) for a, b in pairs])  4.54 us
    ppermute x2, starting transfers between devices, swap(): return lax.ppermute(x, 'row', pairs + [(b, a) for a, b in pairs])  3.76 us
    pallas_call x1, Pallas kernels, on_device(): pl.pallas_call(ends_kernel, grid=(1,), out_shape=ends, in_specs=[one_row(...  1.41 us
    ppermute x1, starting transfers between devices, column_halos(): got = lax.ppermute(jnp.where(low, last, first), 'col', [(0, 1), (1, 0)])  1.3 us
    ppermute x1, waiting for transfers between devices, column_halos(): got = lax.ppermute(jnp.where(low, last, first), 'col', [(0, 1), (1, 0)])  1.06 us
    pallas_call x1, Pallas kernels, on_device(): pl.pallas_call(weights_kernel, grid=(1,), out_shape=weights, in_specs=[wh...  1 us
  transfers between devices with their start and end apart: 3, of which 2 were waited for; matrix products, arithmetic and copies ran while one was open for 0% of the time, Pallas kernels for 3%

profile of v3, /device:TPU:25, one launch (start us, length us, event | category | flops | bytes accessed | tf_op | source)
XLA Modules:
  0.0 30.2 jit_solution(17791914364391722586)
XLA Ops:
  0.0 0.0 copy-start.1
  0.0 0.0 copy-start.2
  0.0 0.0 copy-start.3
  0.0 0.0 copy-start.4
  0.0 0.0 copy-start
  0.0 1.4 %ends.1 = (bf16[2,256,256]{2,1,0:T(8,128)(2,1)S(1)}, f32[2,48,256]{2,1,0:T(8,128)S(1)}) custom-call(bf16[48,256,256]{2,1,0:T(8,128)(2,1)} %after.1, bf16[48,256,256]{2,1,0:T(8,128)(2,1)} %after.1, bf16[48,256,256]{2,1,0:T(8,128)(2,1)} %after.1, bf16[48,256,256]{2,1,0:T(8,128)(2,1)} %after.1), custom_call_target="tpu_custom_call" | custom-call | tf_op jit(solution)/shard_map/ends/pallas_call | solution.py:131
  1.5 0.7 %collective-permute-start.1 = (bf16[256,256]{1,0:T(8,128)(2,1)S(1)}, bf16[256,256]{1,0:T(8,128)(2,1)S(1)}, u32[]{:S(2)}, u32[]{:S(2)}) collective-permute-start(bf16[256,256]{1,0:T(8,128)(2,1)S(1)} %get-tuple-element.11), channel_id=1, source_target_pairs={{0,2},{4,6},{8,10},{12,14},{16,18},{20,22},{24,26},{28,30},{2,0},{... | collective-permute-start | bytes 393224 | tf_op jit(solution)/shard_map/ppermute | solution.py:100
  2.2 3.0 %collective-permute-start = (bf16[256,256]{1,0:T(8,128)(2,1)S(1)}, bf16[256,256]{1,0:T(8,128)(2,1)S(1)}, u32[]{:S(2)}, u32[]{:S(2)}) collective-permute-start(bf16[256,256]{1,0:T(8,128)(2,1)S(1)} %get-tuple-element.12), channel_id=1, source_target_pairs={{2,4},{6,8},{10,12},{14,16},{18,20},{22,24},{26,28},{4,2},{8,6},{1... | collective-permute-start | bytes 393224 | tf_op jit(solution)/shard_map/ppermute | solution.py:100
  5.3 0.1 pad.7.clone
  5.3 0.0 collective-permute-done.1
  5.4 4.5 %collective-permute-done = bf16[256,256]{1,0:T(8,128)(2,1)S(1)} collective-permute-done((bf16[256,256]{1,0:T(8,128)(2,1)S(1)}, bf16[256,256]{1,0:T(8,128)(2,1)S(1)}, u32[]{:S(2)}, u32[]{:S(2)}) %collective-permute-start) | collective-permute-done | bytes 131104 | tf_op jit(solution)/shard_map/ppermute | solution.py:100
  9.9 0.1 maximum_select_fusion
  10.0 1.3 %collective-permute-start.2 = (bf16[64,256]{1,0:T(8,128)(2,1)S(1)}, bf16[64,256]{1,0:T(8,128)(2,1)S(1)}, u32[]{:S(2)}, u32[]{:S(2)}) collective-permute-start(bf16[64,256]{1,0:T(8,128)(2,1)S(1)} %maximum_select_fusion), channel_id=1, source_target_pairs={{0,1},{1,0},{2,3},{3,2},{4,5},{5,4},{6,7},{7,6},{8,9},{9,8},{10,11... | collective-permute-start | bytes 98312 | tf_op jit(solution)/shard_map/ppermute | solution.py:110
  11.3 0.0 copy-done.1
  11.3 0.0 copy-done.2
  11.3 0.0 copy-done.3
  11.3 0.0 copy-done.4
  11.3 1.0 %weights.1.u_ref = bf16[4,768,256]{2,1,0:T(8,128)(2,1)S(1)} custom-call(bf16[256,512]{1,0:T(8,128)(2,1)S(1)} %copy-done.1, f32[3,512]{1,0:T(4,128)S(1)} %copy-done.3, f32[3,512]{1,0:T(4,128)S(1)} %copy-done.4, bf16[512,256]{1,0:T(8,128)(2,1)S(1)} %copy-done.2), custom_call_target="tpu_custom_call" | custom-call | flops 805306368 | bytes 3145728 | tf_op jit(solution)/shard_map/weights/pallas_call | solution.py:145
  12.3 1.1 %collective-permute-done.2 = bf16[64,256]{1,0:T(8,128)(2,1)S(1)} collective-permute-done((bf16[64,256]{1,0:T(8,128)(2,1)S(1)}, bf16[64,256]{1,0:T(8,128)(2,1)S(1)}, u32[]{:S(2)}, u32[]{:S(2)}) %collective-permute-start.2) | collective-permute-done | bytes 32800 | tf_op jit(solution)/shard_map/ppermute | solution.py:110
  13.4 0.0 copy-done
  13.4 16.8 %conv.1 = bf16[48,256,256]{2,1,0:T(8,128)(2,1)} custom-call(bf16[48,256,256]{2,1,0:T(8,128)(2,1)} %after.1, bf16[48,256,256]{2,1,0:T(8,128)(2,1)} %after.1, bf16[48,256,256]{2,1,0:T(8,128)(2,1)} %after.1, bf16[256,256]{1,0:T(8,128)(2,1)S(1)} %get-tuple-element.10.top, bf16[256,256]{1,0:T(8,128)(2,1)S(1)} %get-tuple-element.9.bot, ...), custom_call_target="tpu_custom_call" | custom-call | tf_op jit(solution)/shard_map/conv/pallas_call | solution.py:166
  (7 shorter events, 0.1 us)
Async XLA Ops:
  0.0 11.3 %copy-start.1 = (bf16[256,512]{1,0:T(8,128)(2,1)S(1)}, bf16[256,512]{1,0:T(8,128)(2,1)}, u32[]{:S(2)}) copy-start(bf16[256,512]{1,0:T(8,128)(2,1)} %pin_ref.1) | copy-start | bytes 786436
  0.0 11.3 %copy-start.2 = (bf16[512,256]{1,0:T(8,128)(2,1)S(1)}, bf16[512,256]{1,0:T(8,128)(2,1)}, u32[]{:S(2)}) copy-start(bf16[512,256]{1,0:T(8,128)(2,1)} %po_ref.1) | copy-start | bytes 786436
  0.0 11.3 %copy-start.3 = (f32[3,512]{1,0:T(4,128)S(1)}, f32[3,512]{1,0:T(4,128)}, u32[]{:S(2)}) copy-start(f32[3,512]{1,0:T(4,128)} %tw_ref.1) | copy-start | bytes 18436
  0.0 11.3 %copy-start.4 = (f32[3,512]{1,0:T(4,128)S(1)}, f32[3,512]{1,0:T(4,128)}, u32[]{:S(2)}) copy-start(f32[3,512]{1,0:T(4,128)} %tt_ref.1) | copy-start | bytes 18436
  0.0 13.4 %copy-start = (f32[256]{0:T(256)S(1)}, f32[256]{0:T(256)}, u32[]{:S(2)}) copy-start(f32[256]{0:T(256)} %param.11) | copy-start | bytes 3076
  1.5 3.9 %collective-permute-start.1 = (bf16[256,256]{1,0:T(8,128)(2,1)S(1)}, bf16[256,256]{1,0:T(8,128)(2,1)S(1)}, u32[]{:S(2)}, u32[]{:S(2)}) collective-permute-start(bf16[256,256]{1,0:T(8,128)(2,1)S(1)} %get-tuple-element.11), channel_id=1, source_target_pairs={{0,2},{4,6},{8,10},{12,14},{16,18},{20,22},{24,26},{28,30},{2,0},{... | collective-permute-start | bytes 393224 | tf_op jit(solution)/shard_map/ppermute | solution.py:100
  2.2 7.7 %collective-permute-start = (bf16[256,256]{1,0:T(8,128)(2,1)S(1)}, bf16[256,256]{1,0:T(8,128)(2,1)S(1)}, u32[]{:S(2)}, u32[]{:S(2)}) collective-permute-start(bf16[256,256]{1,0:T(8,128)(2,1)S(1)} %get-tuple-element.12), channel_id=1, source_target_pairs={{2,4},{6,8},{10,12},{14,16},{18,20},{22,24},{26,28},{4,2},{8,6},{1... | collective-permute-start | bytes 393224 | tf_op jit(solution)/shard_map/ppermute | solution.py:100
  10.0 3.4 %collective-permute-start.2 = (bf16[64,256]{1,0:T(8,128)(2,1)S(1)}, bf16[64,256]{1,0:T(8,128)(2,1)S(1)}, u32[]{:S(2)}, u32[]{:S(2)}) collective-permute-start(bf16[64,256]{1,0:T(8,128)(2,1)S(1)} %maximum_select_fusion), channel_id=1, source_target_pairs={{0,1},{1,0},{2,3},{3,2},{4,5},{5,4},{6,7},{7,6},{8,9},{9,8},{10,11... | collective-permute-start | bytes 98312 | tf_op jit(solution)/shard_map/ppermute | solution.py:110

commit v4 on v3

--- a/solution.py
+++ b/solution.py
@@ -8,7 +8,7 @@
 BF16 = jnp.bfloat16
 F32 = jnp.float32
 MIB = 1 << 20
-ROWS = 8
+ROWS = 4
 
 
 def side_columns(x, lead, tail):
@@ -20,44 +20,81 @@
     return left.astype(BF16), right.astype(BF16)
 
 
-def conv_kernel(before, here, after, top, bot, u_ref, lh_ref, rh_ref, bias_ref, out_ref,
-                ends, sides):
+def pair_of_rows(row, r, u_ref):
+    def product(k, a, b, add):
+        sums = [x + y if add else x - y for x, y in zip(row(r + a), row(r + b))]
+        return jnp.dot(jnp.concatenate(sums, axis=1), u_ref[k], preferred_element_type=F32)
+
+    m1 = product(1, 1, 2, True)
+    m2 = product(2, 2, 1, False)
+    m0 = product(0, 0, 2, False)
+    m3 = product(3, 1, 3, False)
+    return m0 + (m1 + m2), (m1 - m2) - m3
+
+
+def finish(centre, half):
+    return (centre.astype(F32) + (half + half * jnp.tanh(half))).astype(BF16)
+
+
+def inner_kernel(before, here, after, u_ref, lh_ref, rh_ref, bias_ref, out_ref, sides):
+    i = pl.program_id(0)
+    n = here.shape[0]
+    bias = bias_ref[...] * 0.5
+
+    def centre(r):
+        return before[0] if r == 0 else after[0] if r > n else here[r - 1]
+
+    def shift(r):
+        at = (i + 1) * n - 1 + r
+        lead, tail = lh_ref[pl.ds(at, 1), :], rh_ref[pl.ds(at, 1), :]
+        sides[r, 0], sides[r, 1] = side_columns(centre(r), lead, tail)
+
+    def row(r):
+        return sides[r, 0], centre(r), sides[r, 1]
+
+    @pl.when(i == 0)
+    def _():
+        shift(0)
+        shift(1)
+
+    @pl.when(i > 0)
+    def _():
+        sides[0:2] = sides[n : n + 2]
+
+    for r in range(0, n, 2):
+        shift(r + 2)
+        shift(r + 3)
+        ya, yb = pair_of_rows(row, r, u_ref)
+        out_ref[r] = finish(here[r], ya + bias)
+        out_ref[r + 1] = finish(here[r + 1], yb + bias)
+
+
+def edge_kernel(here, second, top, bot, u_ref, lh_ref, rh_ref, bias_ref, out_ref, ends, sides):
     i = pl.program_id(0)
     n, w, _ = here.shape
+    base = i * (lh_ref.shape[0] - 16 - n)
     bias = bias_ref[...] * 0.5
+    ends[0] = jnp.where(i == 0, top[0:w, :], second[0])
+    ends[1] = jnp.where(i == 0, second[0], bot[0:w, :])
 
     def centre(r):
         return here[r - 1] if 0 < r <= n else ends[r // n]
 
     def shift(r):
-        at = i * n + r
-        lead, tail = lh_ref[pl.ds(at, 1), :], rh_ref[pl.ds(at, 1), :]
+        lead, tail = lh_ref[pl.ds(base + r, 1), :], rh_ref[pl.ds(base + r, 1), :]
         sides[r, 0], sides[r, 1] = side_columns(centre(r), lead, tail)
 
     def row(r):
         return sides[r, 0], centre(r), sides[r, 1]
 
-    def product(k, a, b, add):
-        sums = [x + y if add else x - y for x, y in zip(row(a), row(b))]
-        return jnp.dot(jnp.concatenate(sums, axis=1), u_ref[k], preferred_element_type=F32)
-
-    def finish(r, half):
-        x = here[r].astype(F32)
-        out_ref[r] = (x + (half + half * jnp.tanh(half))).astype(BF16)
-
-    ends[0] = jnp.where(i == 0, top[...], before[0])
-    ends[1] = jnp.where(i == pl.num_programs(0) - 1, bot[...], after[0])
     shift(0)
     shift(1)
     for r in range(0, n, 2):
         shift(r + 2)
         shift(r + 3)
-        m1 = product(1, r + 1, r + 2, True)
-        m2 = product(2, r + 2, r + 1, False)
-        m0 = product(0, r, r + 2, False)
-        m3 = product(3, r + 1, r + 3, False)
-        finish(r, m0 + (m1 + m2) + bias)
-        finish(r + 1, (m1 - m2) - m3 + bias)
+        ya, yb = pair_of_rows(row, r, u_ref)
+        out_ref[r] = finish(here[r], ya + bias)
+        out_ref[r + 1] = finish(here[r + 1], yb + bias)
 
 
 def ends_kernel(first, last, left, right, rows_ref, cols_ref):
@@ -138,7 +175,13 @@
         compiler_params=params,
         name="ends",
     )(image, image, image, image)
-    top, bot = row_halos(rows[0], rows[1])
+    lh, rh = column_halos(cols[0].astype(BF16), cols[1].astype(BF16))
+
+    def extended(k, at):
+        pad = jnp.zeros((14, c), BF16)
+        return jnp.concatenate([rows[k], lh[at][None], rh[at][None], pad], axis=0)
+
+    top, bot = row_halos(extended(0, 0), extended(1, th - 1))
 
     args = (proj_in, taps_wide, taps_tall, proj_out)
     weights = jax.ShapeDtypeStruct((4, 3 * c, c), BF16)
@@ -155,29 +198,52 @@
         name="weights",
     )(*args)
 
-    def column(k, at):
+    def column(x, at):
         pad = jnp.zeros((14, c), BF16)
-        return jnp.concatenate(
-            [top[at][None], cols[k].astype(BF16), bot[at][None], pad], axis=0)
-
-    lh, rh = column_halos(column(0, 0), column(1, w - 1))
-    small = (top, bot, u, lh.astype(F32), rh.astype(F32), bias.reshape(1, c))
-    block = pl.BlockSpec((n, w, c), lambda i: (i, 0, 0))
-    return pl.pallas_call(
-        conv_kernel,
-        grid=(th // n,),
+        return jnp.concatenate([top[at][None], x, bot[at][None], pad], axis=0).astype(F32)
+
+    def cost(count):
+        return pl.CostEstimate(
+            flops=count * 12 * w * c * c, bytes_accessed=4 * count * w * c,
+            transcendentals=count * w * c)
+
+    bias2 = bias.reshape(1, c)
+    small = (u, lh.astype(F32), rh.astype(F32), bias2)
+    inner = pl.pallas_call(
+        inner_kernel,
+        grid=(th // n - 2,),
         out_shape=jax.ShapeDtypeStruct(image.shape, BF16),
         in_specs=[
-            one_row(lambda i: jnp.maximum(i * n - 1, 0)),
-            block,
-            one_row(lambda i: jnp.minimum(i * n + n, th - 1)),
+            one_row(lambda i: (i + 1) * n - 1),
+            pl.BlockSpec((n, w, c), lambda i: (i + 1, 0, 0)),
+            one_row(lambda i: (i + 2) * n),
             *[whole(x) for x in small],
         ],
-        out_specs=block,
+        out_specs=pl.BlockSpec((n, w, c), lambda i: (i + 1, 0, 0)),
+        scratch_shapes=[pltpu.VMEM((n + 2, 2, w, c), BF16)],
+        compiler_params=params,
+        cost_estimate=cost(th - 2 * n),
+        name="inner",
+    )(image, image, image, *small)
+
+    small = (top, bot, u, column(lh, w), column(rh, w + 1), bias2)
+    edges = pl.pallas_call(
+        edge_kernel,
+        grid=(2,),
+        out_shape=jax.ShapeDtypeStruct((2 * n, w, c), BF16),
+        in_specs=[
+            pl.BlockSpec((n, w, c), lambda i: (i * (th // n - 1), 0, 0)),
+            one_row(lambda i: n + i * (th - 2 * n - 1)),
+            *[whole(x) for x in small],
+        ],
+        out_specs=pl.BlockSpec((n, w, c), lambda i: (i, 0, 0)),
         scratch_shapes=[pltpu.VMEM((2, w, c), BF16), pltpu.VMEM((n + 2, 2, w, c), BF16)],
         compiler_params=params,
-        name="conv",
-    )(image, image, image, *small)
+        cost_estimate=cost(2 * n),
+        name="edges",
+    )(image, image, *small)
+    out = lax.dynamic_update_slice(inner, edges[:n], (0, 0, 0))
+    return lax.dynamic_update_slice(out, edges[n:], (th - n, 0, 0))
 
 
 def solution(mesh):

time: 30.4 us -> 30.5 us (level)
  the two profiles are of different devices: /device:TPU:25 before, /device:TPU:1 now
where the time goes in v4:
time: 30.5 us; the launch traced here: 30 us
  Pallas kernels  20.6 us (68%)
  starting transfers between devices  7.26 us (24%)
  local copies, waits for them, and re-layouts  1.72 us (6%)
    pallas_call x1, Pallas kernels, on_device(): pl.pallas_call(inner_kernel, grid=(th // n - 2,), out_shape=jax.ShapeDtyp...  14.6 us
    ppermute x2, starting transfers between devices, swap(): return lax.ppermute(x, 'row', pairs + [(b, a) for a, b in pairs])  5.13 us
    pallas_call x1, Pallas kernels, on_device(): pl.pallas_call(edge_kernel, grid=(2,), out_shape=jax.ShapeDtypeStruct((2...  3.53 us
    ppermute x1, starting transfers between devices, column_halos(): got = lax.ppermute(jnp.where(low, last, first), 'col', [(0, 1), (1, 0)])  2.13 us
    pallas_call x1, Pallas kernels, on_device(): pl.pallas_call(ends_kernel, grid=(1,), out_shape=ends, in_specs=[one_row(...  1.41 us
    pallas_call x1, Pallas kernels, on_device(): pl.pallas_call(weights_kernel, grid=(1,), out_shape=weights, in_specs=[wh...  1 us
    dynamic_update_slice x1, local copies, waits for them, and re-layouts, on_device(): out = lax.dynamic_update_slice(inner, edges[:n], (0, 0, 0))  0.83 us
    dynamic_update_slice x1, local copies, waits for them, and re-layouts, on_device(): return lax.dynamic_update_slice(out, edges[n:], (th - n, 0, 0))  0.83 us
  transfers between devices with their start and end apart: 3, of which 1 were waited for; matrix products, arithmetic and copies ran while one was open for 0% of the time, Pallas kernels for 52%

profile of v4, /device:TPU:1, one launch (start us, length us, event | category | flops | bytes accessed | tf_op | source)
XLA Modules:
  0.0 30.0 jit_solution(14335304132293561734)
XLA Ops:
  0.0 0.0 copy-start.1
  0.0 0.0 copy-start.2
  0.0 0.0 copy-start.3
  0.0 0.0 copy-start.4
  0.0 0.0 copy-start
  0.0 1.4 %ends.1 = (bf16[2,256,256]{2,1,0:T(8,128)(2,1)S(1)}, f32[2,48,256]{2,1,0:T(8,128)S(1)}) custom-call(bf16[48,256,256]{2,1,0:T(8,128)(2,1)} %second.1, bf16[48,256,256]{2,1,0:T(8,128)(2,1)} %second.1, bf16[48,256,256]{2,1,0:T(8,128)(2,1)} %second.1, bf16[48,256,256]{2,1,0:T(8,128)(2,1)} %second.1), custom_call_target="tpu_custom_call" | custom-call | tf_op jit(solution)/shard_map/ends/pallas_call | solution.py:168
  1.5 2.1 %collective-permute-start = (bf16[48,256]{1,0:T(8,128)(2,1)S(1)}, bf16[48,256]{1,0:T(8,128)(2,1)S(1)}, u32[]{:S(2)}, u32[]{:S(2)}) collective-permute-start(bf16[48,256]{1,0:T(8,128)(2,1)S(1)} %fusion.2), channel_id=1, source_target_pairs={{0,1},{1,0},{2,3},{3,2},{4,5},{5,4},{6,7},{7,6},{8,9},{9,8},{10,11... | collective-permute-start | bytes 73736 | tf_op jit(solution)/shard_map/ppermute | solution.py:147
  3.6 0.0 copy-done.1
  3.6 0.0 copy-done.2
  3.6 0.0 copy-done.3
  3.7 0.0 copy-done.4
  3.7 1.0 %weights.1.u_ref = bf16[4,768,256]{2,1,0:T(8,128)(2,1)S(1)} custom-call(bf16[256,512]{1,0:T(8,128)(2,1)S(1)} %copy-done.1, f32[3,512]{1,0:T(4,128)S(1)} %copy-done.3, f32[3,512]{1,0:T(4,128)S(1)} %copy-done.4, bf16[512,256]{1,0:T(8,128)(2,1)S(1)} %copy-done.2), custom_call_target="tpu_custom_call" | custom-call | flops 805306368 | bytes 3145728 | tf_op jit(solution)/shard_map/weights/pallas_call | solution.py:188
  4.7 0.1 collective-permute-done
  4.9 0.1 broadcast_select_fusion.2
  4.9 1.6 %collective-permute-start.2 = (bf16[272,256]{1,0:T(8,128)(2,1)S(1)}, bf16[272,256]{1,0:T(8,128)(2,1)S(1)}, u32[]{:S(2)}, u32[]{:S(2)}) collective-permute-start(bf16[272,256]{1,0:T(8,128)(2,1)S(1)} %get-tuple-element.15), channel_id=1, source_target_pairs={{0,2},{4,6},{8,10},{12,14},{16,18},{20,22},{24,26},{28,30},{2,0},{... | collective-permute-start | bytes 417800 | tf_op jit(solution)/shard_map/ppermute | solution.py:137
  6.6 3.5 %collective-permute-start.1 = (bf16[272,256]{1,0:T(8,128)(2,1)S(1)}, bf16[272,256]{1,0:T(8,128)(2,1)S(1)}, u32[]{:S(2)}, u32[]{:S(2)}) collective-permute-start(bf16[272,256]{1,0:T(8,128)(2,1)S(1)} %get-tuple-element.16), channel_id=1, source_target_pairs={{2,4},{6,8},{10,12},{14,16},{18,20},{22,24},{26,28},{4,2},{8,6},{1... | collective-permute-start | bytes 417800 | tf_op jit(solution)/shard_map/ppermute | solution.py:137
  10.1 0.0 copy-done
  10.1 14.6 %inner.1 = bf16[48,256,256]{2,1,0:T(8,128)(2,1)} custom-call(bf16[48,256,256]{2,1,0:T(8,128)(2,1)} %second.1, bf16[48,256,256]{2,1,0:T(8,128)(2,1)} %second.1, bf16[48,256,256]{2,1,0:T(8,128)(2,1)} %second.1, bf16[4,768,256]{2,1,0:T(8,128)(2,1)S(1)} %weights.1.u_ref, f32[48,256]{1,0:T(8,128)S(1)} %get-tuple-element.27.lh_ref, ...), custom_call_target="tpu_custom_call" | custom-call | flops 8053063680 | bytes 10485760 | tf_op jit(solution)/shard_map/inner/pallas_call | solution.py:212
  24.7 0.0 collective-permute-done.2
  24.7 0.0 collective-permute-done.1
  24.8 3.5 %edges.1 = bf16[8,256,256]{2,1,0:T(8,128)(2,1)S(1)} custom-call(bf16[48,256,256]{2,1,0:T(8,128)(2,1)} %second.1, bf16[48,256,256]{2,1,0:T(8,128)(2,1)} %second.1, bf16[272,256]{1,0:T(8,128)(2,1)S(1)} %get-tuple-element.14.top, bf16[272,256]{1,0:T(8,128)(2,1)S(1)} %get-tuple-element.13.bot, bf16[4,768,256]{2,1,0:T(8,128)(2,1)S(1)} %weights.1.u_ref, ...), custom_call_target="tpu_custom_call" | custom-call | flops 1610612736 | bytes 2097152 | tf_op jit(solution)/shard_map/edges/pallas_call | solution.py:230
  28.4 0.8 %slice_dynamic-update-slice_fusion.1 = bf16[48,256,256]{2,1,0:T(8,128)(2,1)} fusion(bf16[48,256,256]{2,1,0:T(8,128)(2,1)} %inner.1, bf16[8,256,256]{2,1,0:T(8,128)(2,1)S(1)} %edges.1), kind=kLoop, calls=%fused_computation.1 | loop fusion | bytes 1048576 | tf_op jit(solution)/shard_map/dynamic_update_slice | solution.py:245
  29.2 0.8 %slice_dynamic-update-slice_fusion = bf16[48,256,256]{2,1,0:T(8,128)(2,1)} fusion(bf16[48,256,256]{2,1,0:T(8,128)(2,1)} %slice_dynamic-update-slice_fusion.1, bf16[8,256,256]{2,1,0:T(8,128)(2,1)S(1)} %edges.1), kind=kLoop, calls=%fused_computation | loop fusion | bytes 1048576 | tf_op jit(solution)/shard_map/dynamic_update_slice | solution.py:246
  (10 shorter events, 0.1 us)
Async XLA Ops:
  0.0 3.6 %copy-start.1 = (bf16[256,512]{1,0:T(8,128)(2,1)S(1)}, bf16[256,512]{1,0:T(8,128)(2,1)}, u32[]{:S(2)}) copy-start(bf16[256,512]{1,0:T(8,128)(2,1)} %pin_ref.1) | copy-start | bytes 786436
  0.0 3.6 %copy-start.2 = (bf16[512,256]{1,0:T(8,128)(2,1)S(1)}, bf16[512,256]{1,0:T(8,128)(2,1)}, u32[]{:S(2)}) copy-start(bf16[512,256]{1,0:T(8,128)(2,1)} %po_ref.1) | copy-start | bytes 786436
  0.0 3.6 %copy-start.3 = (f32[3,512]{1,0:T(4,128)S(1)}, f32[3,512]{1,0:T(4,128)}, u32[]{:S(2)}) copy-start(f32[3,512]{1,0:T(4,128)} %tw_ref.1) | copy-start | bytes 18436
  0.0 3.7 %copy-start.4 = (f32[3,512]{1,0:T(4,128)S(1)}, f32[3,512]{1,0:T(4,128)}, u32[]{:S(2)}) copy-start(f32[3,512]{1,0:T(4,128)} %tt_ref.1) | copy-start | bytes 18436
  0.0 10.1 %copy-start = (f32[256]{0:T(256)S(1)}, f32[256]{0:T(256)}, u32[]{:S(2)}) copy-start(f32[256]{0:T(256)} %param.11) | copy-start | bytes 3076
  1.5 3.4 %collective-permute-start = (bf16[48,256]{1,0:T(8,128)(2,1)S(1)}, bf16[48,256]{1,0:T(8,128)(2,1)S(1)}, u32[]{:S(2)}, u32[]{:S(2)}) collective-permute-start(bf16[48,256]{1,0:T(8,128)(2,1)S(1)} %fusion.2), channel_id=1, source_target_pairs={{0,1},{1,0},{2,3},{3,2},{4,5},{5,4},{6,7},{7,6},{8,9},{9,8},{10,11... | collective-permute-start | bytes 73736 | tf_op jit(solution)/shard_map/ppermute | solution.py:147
  4.9 19.8 %collective-permute-start.2 = (bf16[272,256]{1,0:T(8,128)(2,1)S(1)}, bf16[272,256]{1,0:T(8,128)(2,1)S(1)}, u32[]{:S(2)}, u32[]{:S(2)}) collective-permute-start(bf16[272,256]{1,0:T(8,128)(2,1)S(1)} %get-tuple-element.15), channel_id=1, source_target_pairs={{0,2},{4,6},{8,10},{12,14},{16,18},{20,22},{24,26},{28,30},{2,0},{... | collective-permute-start | bytes 417800 | tf_op jit(solution)/shard_map/ppermute | solution.py:137
  6.6 18.2 %collective-permute-start.1 = (bf16[272,256]{1,0:T(8,128)(2,1)S(1)}, bf16[272,256]{1,0:T(8,128)(2,1)S(1)}, u32[]{:S(2)}, u32[]{:S(2)}) collective-permute-start(bf16[272,256]{1,0:T(8,128)(2,1)S(1)} %get-tuple-element.16), channel_id=1, source_target_pairs={{2,4},{6,8},{10,12},{14,16},{18,20},{22,24},{26,28},{4,2},{8,6},{1... | collective-permute-start | bytes 417800 | tf_op jit(solution)/shard_map/ppermute | solution.py:137

commit v5 on v3

--- a/solution.py
+++ b/solution.py
@@ -11,13 +11,14 @@
 ROWS = 8
 
 
-def side_columns(x, lead, tail):
+def side_columns(x, lead, tail, left_ref, right_ref):
     w = x.shape[0]
-    at = lax.broadcasted_iota(jnp.int32, x.shape, 0)
-    x32 = x.astype(F32)
-    left = jnp.where(at == 0, lead, pltpu.roll(x32, 1, 0))
-    right = jnp.where(at == w - 1, tail, pltpu.roll(x32, w - 1, 0))
-    return left.astype(BF16), right.astype(BF16)
+    left, right = pltpu.roll(x, 1, 0), pltpu.roll(x, w - 1, 0)
+    at = lax.broadcasted_iota(jnp.int32, (16, x.shape[1]), 0)
+    left_ref[16:w] = left[16:]
+    left_ref[0:16] = jnp.where(at == 0, lead, left[:16].astype(F32)).astype(BF16)
+    right_ref[0 : w - 16] = right[: w - 16]
+    right_ref[w - 16 : w] = jnp.where(at == 15, tail, right[w - 16 :].astype(F32)).astype(BF16)
 
 
 def conv_kernel(before, here, after, top, bot, u_ref, lh_ref, rh_ref, bias_ref, out_ref,
@@ -32,7 +33,7 @@
     def shift(r):
         at = i * n + r
         lead, tail = lh_ref[pl.ds(at, 1), :], rh_ref[pl.ds(at, 1), :]
-        sides[r, 0], sides[r, 1] = side_columns(centre(r), lead, tail)
+        side_columns(centre(r), lead, tail, sides.at[r, 0], sides.at[r, 1])
 
     def row(r):
         return sides[r, 0], centre(r), sides[r, 1]

time: 30.4 us -> 30.4 us (level)
  no operation moved by 1% of the time
where the time goes in v5:
time: 30.4 us; the launch traced here: 30.2 us
  Pallas kernels  19.2 us (63%)
  waiting for transfers between devices  5.6 us (18%)
  starting transfers between devices  5.06 us (17%)
    pallas_call x1, Pallas kernels, on_device(): pl.pallas_call(conv_kernel, grid=(th // n,), out_shape=jax.ShapeDtypeStru...  16.8 us
    ppermute x2, waiting for transfers between devices, swap(): return lax.ppermute(x, 'row', pairs + [(b, a) for a, b in pairs])  4.54 us
    ppermute x2, starting transfers between devices, swap(): return lax.ppermute(x, 'row', pairs + [(b, a) for a, b in pairs])  3.76 us
    pallas_call x1, Pallas kernels, on_device(): pl.pallas_call(ends_kernel, grid=(1,), out_shape=ends, in_specs=[one_row(...  1.41 us
    ppermute x1, starting transfers between devices, column_halos(): got = lax.ppermute(jnp.where(low, last, first), 'col', [(0, 1), (1, 0)])  1.3 us
    ppermute x1, waiting for transfers between devices, column_halos(): got = lax.ppermute(jnp.where(low, last, first), 'col', [(0, 1), (1, 0)])  1.06 us
    pallas_call x1, Pallas kernels, on_device(): pl.pallas_call(weights_kernel, grid=(1,), out_shape=weights, in_specs=[wh...  1 us
  transfers between devices with their start and end apart: 3, of which 2 were waited for; matrix products, arithmetic and copies ran while one was open for 0% of the time, Pallas kernels for 3%

profile of v5, /device:TPU:25, one launch (start us, length us, event | category | flops | bytes accessed | tf_op | source)
XLA Modules:
  0.0 30.2 jit_solution(14905621220281587367)
XLA Ops:
  0.0 0.0 copy-start.1
  0.0 0.0 copy-start.2
  0.0 0.0 copy-start.3
  0.0 0.0 copy-start.4
  0.0 0.0 copy-start
  0.0 1.4 %ends.1 = (bf16[2,256,256]{2,1,0:T(8,128)(2,1)S(1)}, f32[2,48,256]{2,1,0:T(8,128)S(1)}) custom-call(bf16[48,256,256]{2,1,0:T(8,128)(2,1)} %after.1, bf16[48,256,256]{2,1,0:T(8,128)(2,1)} %after.1, bf16[48,256,256]{2,1,0:T(8,128)(2,1)} %after.1, bf16[48,256,256]{2,1,0:T(8,128)(2,1)} %after.1), custom_call_target="tpu_custom_call" | custom-call | tf_op jit(solution)/shard_map/ends/pallas_call | solution.py:132
  1.5 0.7 %collective-permute-start.1 = (bf16[256,256]{1,0:T(8,128)(2,1)S(1)}, bf16[256,256]{1,0:T(8,128)(2,1)S(1)}, u32[]{:S(2)}, u32[]{:S(2)}) collective-permute-start(bf16[256,256]{1,0:T(8,128)(2,1)S(1)} %get-tuple-element.11), channel_id=1, source_target_pairs={{0,2},{4,6},{8,10},{12,14},{16,18},{20,22},{24,26},{28,30},{2,0},{... | collective-permute-start | bytes 393224 | tf_op jit(solution)/shard_map/ppermute | solution.py:101
  2.2 3.0 %collective-permute-start = (bf16[256,256]{1,0:T(8,128)(2,1)S(1)}, bf16[256,256]{1,0:T(8,128)(2,1)S(1)}, u32[]{:S(2)}, u32[]{:S(2)}) collective-permute-start(bf16[256,256]{1,0:T(8,128)(2,1)S(1)} %get-tuple-element.12), channel_id=1, source_target_pairs={{2,4},{6,8},{10,12},{14,16},{18,20},{22,24},{26,28},{4,2},{8,6},{1... | collective-permute-start | bytes 393224 | tf_op jit(solution)/shard_map/ppermute | solution.py:101
  5.3 0.1 pad.7.clone
  5.3 0.0 collective-permute-done.1
  5.4 4.5 %collective-permute-done = bf16[256,256]{1,0:T(8,128)(2,1)S(1)} collective-permute-done((bf16[256,256]{1,0:T(8,128)(2,1)S(1)}, bf16[256,256]{1,0:T(8,128)(2,1)S(1)}, u32[]{:S(2)}, u32[]{:S(2)}) %collective-permute-start) | collective-permute-done | bytes 131104 | tf_op jit(solution)/shard_map/ppermute | solution.py:101
  9.9 0.1 maximum_select_fusion
  10.0 1.3 %collective-permute-start.2 = (bf16[64,256]{1,0:T(8,128)(2,1)S(1)}, bf16[64,256]{1,0:T(8,128)(2,1)S(1)}, u32[]{:S(2)}, u32[]{:S(2)}) collective-permute-start(bf16[64,256]{1,0:T(8,128)(2,1)S(1)} %maximum_select_fusion), channel_id=1, source_target_pairs={{0,1},{1,0},{2,3},{3,2},{4,5},{5,4},{6,7},{7,6},{8,9},{9,8},{10,11... | collective-permute-start | bytes 98312 | tf_op jit(solution)/shard_map/ppermute | solution.py:111
  11.3 0.0 copy-done.1
  11.3 0.0 copy-done.2
  11.3 0.0 copy-done.3
  11.3 0.0 copy-done.4
  11.3 1.0 %weights.1.u_ref = bf16[4,768,256]{2,1,0:T(8,128)(2,1)S(1)} custom-call(bf16[256,512]{1,0:T(8,128)(2,1)S(1)} %copy-done.1, f32[3,512]{1,0:T(4,128)S(1)} %copy-done.3, f32[3,512]{1,0:T(4,128)S(1)} %copy-done.4, bf16[512,256]{1,0:T(8,128)(2,1)S(1)} %copy-done.2), custom_call_target="tpu_custom_call" | custom-call | flops 805306368 | bytes 3145728 | tf_op jit(solution)/shard_map/weights/pallas_call | solution.py:146
  12.3 1.1 %collective-permute-done.2 = bf16[64,256]{1,0:T(8,128)(2,1)S(1)} collective-permute-done((bf16[64,256]{1,0:T(8,128)(2,1)S(1)}, bf16[64,256]{1,0:T(8,128)(2,1)S(1)}, u32[]{:S(2)}, u32[]{:S(2)}) %collective-permute-start.2) | collective-permute-done | bytes 32800 | tf_op jit(solution)/shard_map/ppermute | solution.py:111
  13.4 0.0 copy-done
  13.4 16.8 %conv.1 = bf16[48,256,256]{2,1,0:T(8,128)(2,1)} custom-call(bf16[48,256,256]{2,1,0:T(8,128)(2,1)} %after.1, bf16[48,256,256]{2,1,0:T(8,128)(2,1)} %after.1, bf16[48,256,256]{2,1,0:T(8,128)(2,1)} %after.1, bf16[256,256]{1,0:T(8,128)(2,1)S(1)} %get-tuple-element.10.top, bf16[256,256]{1,0:T(8,128)(2,1)S(1)} %get-tuple-element.9.bot, ...), custom_call_target="tpu_custom_call" | custom-call | tf_op jit(solution)/shard_map/conv/pallas_call | solution.py:167
  (7 shorter events, 0.1 us)
Async XLA Ops:
  0.0 11.3 %copy-start.1 = (bf16[256,512]{1,0:T(8,128)(2,1)S(1)}, bf16[256,512]{1,0:T(8,128)(2,1)}, u32[]{:S(2)}) copy-start(bf16[256,512]{1,0:T(8,128)(2,1)} %pin_ref.1) | copy-start | bytes 786436
  0.0 11.3 %copy-start.2 = (bf16[512,256]{1,0:T(8,128)(2,1)S(1)}, bf16[512,256]{1,0:T(8,128)(2,1)}, u32[]{:S(2)}) copy-start(bf16[512,256]{1,0:T(8,128)(2,1)} %po_ref.1) | copy-start | bytes 786436
  0.0 11.3 %copy-start.3 = (f32[3,512]{1,0:T(4,128)S(1)}, f32[3,512]{1,0:T(4,128)}, u32[]{:S(2)}) copy-start(f32[3,512]{1,0:T(4,128)} %tw_ref.1) | copy-start | bytes 18436
  0.0 11.3 %copy-start.4 = (f32[3,512]{1,0:T(4,128)S(1)}, f32[3,512]{1,0:T(4,128)}, u32[]{:S(2)}) copy-start(f32[3,512]{1,0:T(4,128)} %tt_ref.1) | copy-start | bytes 18436
  0.0 13.4 %copy-start = (f32[256]{0:T(256)S(1)}, f32[256]{0:T(256)}, u32[]{:S(2)}) copy-start(f32[256]{0:T(256)} %param.11) | copy-start | bytes 3076
  1.5 3.9 %collective-permute-start.1 = (bf16[256,256]{1,0:T(8,128)(2,1)S(1)}, bf16[256,256]{1,0:T(8,128)(2,1)S(1)}, u32[]{:S(2)}, u32[]{:S(2)}) collective-permute-start(bf16[256,256]{1,0:T(8,128)(2,1)S(1)} %get-tuple-element.11), channel_id=1, source_target_pairs={{0,2},{4,6},{8,10},{12,14},{16,18},{20,22},{24,26},{28,30},{2,0},{... | collective-permute-start | bytes 393224 | tf_op jit(solution)/shard_map/ppermute | solution.py:101
  2.2 7.7 %collective-permute-start = (bf16[256,256]{1,0:T(8,128)(2,1)S(1)}, bf16[256,256]{1,0:T(8,128)(2,1)S(1)}, u32[]{:S(2)}, u32[]{:S(2)}) collective-permute-start(bf16[256,256]{1,0:T(8,128)(2,1)S(1)} %get-tuple-element.12), channel_id=1, source_target_pairs={{2,4},{6,8},{10,12},{14,16},{18,20},{22,24},{26,28},{4,2},{8,6},{1... | collective-permute-start | bytes 393224 | tf_op jit(solution)/shard_map/ppermute | solution.py:101
  10.0 3.4 %collective-permute-start.2 = (bf16[64,256]{1,0:T(8,128)(2,1)S(1)}, bf16[64,256]{1,0:T(8,128)(2,1)S(1)}, u32[]{:S(2)}, u32[]{:S(2)}) collective-permute-start(bf16[64,256]{1,0:T(8,128)(2,1)S(1)} %maximum_select_fusion), channel_id=1, source_target_pairs={{0,1},{1,0},{2,3},{3,2},{4,5},{5,4},{6,7},{7,6},{8,9},{9,8},{10,11... | collective-permute-start | bytes 98312 | tf_op jit(solution)/shard_map/ppermute | solution.py:111

commit v6 on v5

--- a/solution.py
+++ b/solution.py
@@ -11,18 +11,19 @@
 ROWS = 8
 
 
-def side_columns(x, lead, tail, left_ref, right_ref):
+def with_sides(x, lead, tail):
     w = x.shape[0]
     left, right = pltpu.roll(x, 1, 0), pltpu.roll(x, w - 1, 0)
     at = lax.broadcasted_iota(jnp.int32, (16, x.shape[1]), 0)
-    left_ref[16:w] = left[16:]
-    left_ref[0:16] = jnp.where(at == 0, lead, left[:16].astype(F32)).astype(BF16)
-    right_ref[0 : w - 16] = right[: w - 16]
-    right_ref[w - 16 : w] = jnp.where(at == 15, tail, right[w - 16 :].astype(F32)).astype(BF16)
+    head = jnp.where(at == 0, lead, left[:16].astype(F32)).astype(BF16)
+    foot = jnp.where(at == 15, tail, right[w - 16 :].astype(F32)).astype(BF16)
+    left = jnp.concatenate([head, left[16:]], axis=0)
+    right = jnp.concatenate([right[: w - 16], foot], axis=0)
+    return jnp.concatenate([left, x, right], axis=1)
 
 
 def conv_kernel(before, here, after, top, bot, u_ref, lh_ref, rh_ref, bias_ref, out_ref,
-                ends, sides):
+                ends):
     i = pl.program_id(0)
     n, w, _ = here.shape
     bias = bias_ref[...] * 0.5
@@ -30,17 +31,15 @@
     def centre(r):
         return here[r - 1] if 0 < r <= n else ends[r // n]
 
-    def shift(r):
-        at = i * n + r
-        lead, tail = lh_ref[pl.ds(at, 1), :], rh_ref[pl.ds(at, 1), :]
-        side_columns(centre(r), lead, tail, sides.at[r, 0], sides.at[r, 1])
+    def product(k, a, b, add):
+        def both(x, y):
+            return x + y if add else x - y
 
-    def row(r):
-        return sides[r, 0], centre(r), sides[r, 1]
-
-    def product(k, a, b, add):
-        sums = [x + y if add else x - y for x, y in zip(row(a), row(b))]
-        return jnp.dot(jnp.concatenate(sums, axis=1), u_ref[k], preferred_element_type=F32)
+        lead, tail = [
+            both(ref[pl.ds(i * n + a, 1), :], ref[pl.ds(i * n + b, 1), :]) for ref in (lh_ref, rh_ref)
+        ]
+        lhs = with_sides(both(centre(a), centre(b)), lead, tail)
+        return jnp.dot(lhs, u_ref[k], preferred_element_type=F32)
 
     def finish(r, half):
         x = here[r].astype(F32)
@@ -48,11 +47,7 @@
 
     ends[0] = jnp.where(i == 0, top[...], before[0])
     ends[1] = jnp.where(i == pl.num_programs(0) - 1, bot[...], after[0])
-    shift(0)
-    shift(1)
     for r in range(0, n, 2):
-        shift(r + 2)
-        shift(r + 3)
         m1 = product(1, r + 1, r + 2, True)
         m2 = product(2, r + 2, r + 1, False)
         m0 = product(0, r, r + 2, False)
@@ -175,7 +170,7 @@
             *[whole(x) for x in small],
         ],
         out_specs=block,
-        scratch_shapes=[pltpu.VMEM((2, w, c), BF16), pltpu.VMEM((n + 2, 2, w, c), BF16)],
+        scratch_shapes=[pltpu.VMEM((2, w, c), BF16)],
         compiler_params=params,
         name="conv",
     )(image, image, image, *small)

time: 30.4 us -> 29.8 us (0.980)
  Pallas kernels: 19.2 us -> 18.6 us
    pallas_call x1, Pallas kernels: 16.8 us -> 16.2 us  [on_device(): pl.pallas_call(conv_kernel, grid=(th // n,), out_shape=jax.ShapeDtypeStru...]
where the time goes in v6:
time: 29.8 us; the launch traced here: 29.7 us
  Pallas kernels  18.6 us (62%)
  waiting for transfers between devices  5.6 us (19%)
  starting transfers between devices  5.06 us (17%)
    pallas_call x1, Pallas kernels, on_device(): pl.pallas_call(conv_kernel, grid=(th // n,), out_shape=jax.ShapeDtypeStru...  16.2 us
    ppermute x2, waiting for transfers between devices, swap(): return lax.ppermute(x, 'row', pairs + [(b, a) for a, b in pairs])  4.54 us
    ppermute x2, starting transfers between devices, swap(): return lax.ppermute(x, 'row', pairs + [(b, a) for a, b in pairs])  3.76 us
    pallas_call x1, Pallas kernels, on_device(): pl.pallas_call(ends_kernel, grid=(1,), out_shape=ends, in_specs=[one_row(...  1.41 us
    ppermute x1, starting transfers between devices, column_halos(): got = lax.ppermute(jnp.where(low, last, first), 'col', [(0, 1), (1, 0)])  1.3 us
    ppermute x1, waiting for transfers between devices, column_halos(): got = lax.ppermute(jnp.where(low, last, first), 'col', [(0, 1), (1, 0)])  1.06 us
    pallas_call x1, Pallas kernels, on_device(): pl.pallas_call(weights_kernel, grid=(1,), out_shape=weights, in_specs=[wh...  1 us
  transfers between devices with their start and end apart: 3, of which 2 were waited for; matrix products, arithmetic and copies ran while one was open for 0% of the time, Pallas kernels for 3%

profile of v6, /device:TPU:25, one launch (start us, length us, event | category | flops | bytes accessed | tf_op | source)
XLA Modules:
  0.0 29.7 jit_solution(8630379155834776197)
XLA Ops:
  0.0 0.0 copy-start.1
  0.0 0.0 copy-start.2
  0.0 0.0 copy-start.3
  0.0 0.0 copy-start.4
  0.0 0.0 copy-start
  0.0 1.4 %ends.1 = (bf16[2,256,256]{2,1,0:T(8,128)(2,1)S(1)}, f32[2,48,256]{2,1,0:T(8,128)S(1)}) custom-call(bf16[48,256,256]{2,1,0:T(8,128)(2,1)} %after.1, bf16[48,256,256]{2,1,0:T(8,128)(2,1)} %after.1, bf16[48,256,256]{2,1,0:T(8,128)(2,1)} %after.1, bf16[48,256,256]{2,1,0:T(8,128)(2,1)} %after.1), custom_call_target="tpu_custom_call" | custom-call | tf_op jit(solution)/shard_map/ends/pallas_call | solution.py:127
  1.5 0.7 %collective-permute-start.1 = (bf16[256,256]{1,0:T(8,128)(2,1)S(1)}, bf16[256,256]{1,0:T(8,128)(2,1)S(1)}, u32[]{:S(2)}, u32[]{:S(2)}) collective-permute-start(bf16[256,256]{1,0:T(8,128)(2,1)S(1)} %get-tuple-element.11), channel_id=1, source_target_pairs={{0,2},{4,6},{8,10},{12,14},{16,18},{20,22},{24,26},{28,30},{2,0},{... | collective-permute-start | bytes 393224 | tf_op jit(solution)/shard_map/ppermute | solution.py:96
  2.2 3.0 %collective-permute-start = (bf16[256,256]{1,0:T(8,128)(2,1)S(1)}, bf16[256,256]{1,0:T(8,128)(2,1)S(1)}, u32[]{:S(2)}, u32[]{:S(2)}) collective-permute-start(bf16[256,256]{1,0:T(8,128)(2,1)S(1)} %get-tuple-element.12), channel_id=1, source_target_pairs={{2,4},{6,8},{10,12},{14,16},{18,20},{22,24},{26,28},{4,2},{8,6},{1... | collective-permute-start | bytes 393224 | tf_op jit(solution)/shard_map/ppermute | solution.py:96
  5.3 0.1 pad.7.clone
  5.3 0.0 collective-permute-done.1
  5.4 4.5 %collective-permute-done = bf16[256,256]{1,0:T(8,128)(2,1)S(1)} collective-permute-done((bf16[256,256]{1,0:T(8,128)(2,1)S(1)}, bf16[256,256]{1,0:T(8,128)(2,1)S(1)}, u32[]{:S(2)}, u32[]{:S(2)}) %collective-permute-start) | collective-permute-done | bytes 131104 | tf_op jit(solution)/shard_map/ppermute | solution.py:96
  9.9 0.1 maximum_select_fusion
  10.0 1.3 %collective-permute-start.2 = (bf16[64,256]{1,0:T(8,128)(2,1)S(1)}, bf16[64,256]{1,0:T(8,128)(2,1)S(1)}, u32[]{:S(2)}, u32[]{:S(2)}) collective-permute-start(bf16[64,256]{1,0:T(8,128)(2,1)S(1)} %maximum_select_fusion), channel_id=1, source_target_pairs={{0,1},{1,0},{2,3},{3,2},{4,5},{5,4},{6,7},{7,6},{8,9},{9,8},{10,11... | collective-permute-start | bytes 98312 | tf_op jit(solution)/shard_map/ppermute | solution.py:106
  11.3 0.0 copy-done.1
  11.3 0.0 copy-done.2
  11.3 0.0 copy-done.3
  11.3 0.0 copy-done.4
  11.3 1.0 %weights.1.u_ref = bf16[4,768,256]{2,1,0:T(8,128)(2,1)S(1)} custom-call(bf16[256,512]{1,0:T(8,128)(2,1)S(1)} %copy-done.1, f32[3,512]{1,0:T(4,128)S(1)} %copy-done.3, f32[3,512]{1,0:T(4,128)S(1)} %copy-done.4, bf16[512,256]{1,0:T(8,128)(2,1)S(1)} %copy-done.2), custom_call_target="tpu_custom_call" | custom-call | flops 805306368 | bytes 3145728 | tf_op jit(solution)/shard_map/weights/pallas_call | solution.py:141
  12.3 1.1 %collective-permute-done.2 = bf16[64,256]{1,0:T(8,128)(2,1)S(1)} collective-permute-done((bf16[64,256]{1,0:T(8,128)(2,1)S(1)}, bf16[64,256]{1,0:T(8,128)(2,1)S(1)}, u32[]{:S(2)}, u32[]{:S(2)}) %collective-permute-start.2) | collective-permute-done | bytes 32800 | tf_op jit(solution)/shard_map/ppermute | solution.py:106
  13.4 0.0 copy-done
  13.4 16.2 %conv.1 = bf16[48,256,256]{2,1,0:T(8,128)(2,1)} custom-call(bf16[48,256,256]{2,1,0:T(8,128)(2,1)} %after.1, bf16[48,256,256]{2,1,0:T(8,128)(2,1)} %after.1, bf16[48,256,256]{2,1,0:T(8,128)(2,1)} %after.1, bf16[256,256]{1,0:T(8,128)(2,1)S(1)} %get-tuple-element.10.top, bf16[256,256]{1,0:T(8,128)(2,1)S(1)} %get-tuple-element.9.bot, ...), custom_call_target="tpu_custom_call" | custom-call | tf_op jit(solution)/shard_map/conv/pallas_call | solution.py:162
  (7 shorter events, 0.1 us)
Async XLA Ops:
  0.0 11.3 %copy-start.1 = (bf16[256,512]{1,0:T(8,128)(2,1)S(1)}, bf16[256,512]{1,0:T(8,128)(2,1)}, u32[]{:S(2)}) copy-start(bf16[256,512]{1,0:T(8,128)(2,1)} %pin_ref.1) | copy-start | bytes 786436
  0.0 11.3 %copy-start.2 = (bf16[512,256]{1,0:T(8,128)(2,1)S(1)}, bf16[512,256]{1,0:T(8,128)(2,1)}, u32[]{:S(2)}) copy-start(bf16[512,256]{1,0:T(8,128)(2,1)} %po_ref.1) | copy-start | bytes 786436
  0.0 11.3 %copy-start.3 = (f32[3,512]{1,0:T(4,128)S(1)}, f32[3,512]{1,0:T(4,128)}, u32[]{:S(2)}) copy-start(f32[3,512]{1,0:T(4,128)} %tw_ref.1) | copy-start | bytes 18436
  0.0 11.3 %copy-start.4 = (f32[3,512]{1,0:T(4,128)S(1)}, f32[3,512]{1,0:T(4,128)}, u32[]{:S(2)}) copy-start(f32[3,512]{1,0:T(4,128)} %tt_ref.1) | copy-start | bytes 18436
  0.0 13.4 %copy-start = (f32[256]{0:T(256)S(1)}, f32[256]{0:T(256)}, u32[]{:S(2)}) copy-start(f32[256]{0:T(256)} %param.11) | copy-start | bytes 3076
  1.5 3.9 %collective-permute-start.1 = (bf16[256,256]{1,0:T(8,128)(2,1)S(1)}, bf16[256,256]{1,0:T(8,128)(2,1)S(1)}, u32[]{:S(2)}, u32[]{:S(2)}) collective-permute-start(bf16[256,256]{1,0:T(8,128)(2,1)S(1)} %get-tuple-element.11), channel_id=1, source_target_pairs={{0,2},{4,6},{8,10},{12,14},{16,18},{20,22},{24,26},{28,30},{2,0},{... | collective-permute-start | bytes 393224 | tf_op jit(solution)/shard_map/ppermute | solution.py:96
  2.2 7.7 %collective-permute-start = (bf16[256,256]{1,0:T(8,128)(2,1)S(1)}, bf16[256,256]{1,0:T(8,128)(2,1)S(1)}, u32[]{:S(2)}, u32[]{:S(2)}) collective-permute-start(bf16[256,256]{1,0:T(8,128)(2,1)S(1)} %get-tuple-element.12), channel_id=1, source_target_pairs={{2,4},{6,8},{10,12},{14,16},{18,20},{22,24},{26,28},{4,2},{8,6},{1... | collective-permute-start | bytes 393224 | tf_op jit(solution)/shard_map/ppermute | solution.py:96
  10.0 3.4 %collective-permute-start.2 = (bf16[64,256]{1,0:T(8,128)(2,1)S(1)}, bf16[64,256]{1,0:T(8,128)(2,1)S(1)}, u32[]{:S(2)}, u32[]{:S(2)}) collective-permute-start(bf16[64,256]{1,0:T(8,128)(2,1)S(1)} %maximum_select_fusion), channel_id=1, source_target_pairs={{0,1},{1,0},{2,3},{3,2},{4,5},{5,4},{6,7},{7,6},{8,9},{9,8},{10,11... | collective-permute-start | bytes 98312 | tf_op jit(solution)/shard_map/ppermute | solution.py:106

commit v7 on v6

--- a/solution.py
+++ b/solution.py
@@ -85,27 +85,41 @@
     return lax.ppermute(x, axis, [(i + 1, i) for i in range(count - 1)])
 
 
+def row_swap(x, start, cross=False):
+    ends = range(start, lax.axis_size("row") - 1, 2)
+    pairs = [(i, i + 1) for i in ends]
+    axis = "row"
+    if cross:
+        pairs = [(2 * i + k, 2 * (i + 1) + 1 - k) for i in ends for k in range(2)]
+        axis = ("row", "col")
+    return lax.ppermute(x, axis, pairs + [(b, a) for a, b in pairs])
+
+
 def row_halos(first, last):
-    count = lax.axis_size("row")
-    if count % 2:
+    if lax.axis_size("row") % 2:
         return shifted(last, "row", 1), shifted(first, "row", -1)
     even = lax.axis_index("row") % 2 == 0
-
-    def swap(x, start):
-        pairs = [(i, i + 1) for i in range(start, count - 1, 2)]
-        return lax.ppermute(x, "row", pairs + [(b, a) for a, b in pairs])
-
-    got = swap(jnp.where(even, last, first), 0)
-    far = swap(jnp.where(even, first, last), 1)
+    got = row_swap(jnp.where(even, last, first), 0)
+    far = row_swap(jnp.where(even, first, last), 1)
     return jnp.where(even, far, got), jnp.where(even, got, far)
 
 
+def columns_of_two(first, last):
+    even, low = lax.axis_index("row") % 2 == 0, lax.axis_index("col") == 0
+    side = jnp.where(low, last, first)
+    head, foot = side[:16], side[-16:]
+    mid = lax.ppermute(side, "col", [(0, 1), (1, 0)])
+    got = row_swap(jnp.where(even, foot, head), 0, True)
+    far = row_swap(jnp.where(even, head, foot), 1, True)
+    up = jnp.where(even, far[15:], got[15:])
+    down = jnp.where(even, got[:1], far[:1])
+    pad = jnp.zeros((14, side.shape[1]), BF16)
+    column = jnp.concatenate([up, mid, down, pad], axis=0).astype(F32)
+    zero = jnp.zeros_like(column)
+    return jnp.where(low, zero, column), jnp.where(low, column, zero)
+
+
 def column_halos(first, last):
-    if lax.axis_size("col") == 2:
-        low = lax.axis_index("col") == 0
-        got = lax.ppermute(jnp.where(low, last, first), "col", [(0, 1), (1, 0)])
-        zero = jnp.zeros_like(got)
-        return jnp.where(low, zero, got), jnp.where(low, got, zero)
     return shifted(last, "col", 1), shifted(first, "col", -1)
 
 
@@ -156,7 +170,10 @@
         return jnp.concatenate(
             [top[at][None], cols[k].astype(BF16), bot[at][None], pad], axis=0)
 
-    lh, rh = column_halos(column(0, 0), column(1, w - 1))
+    if lax.axis_size("col") == 2 and lax.axis_size("row") % 2 == 0:
+        lh, rh = columns_of_two(cols[0].astype(BF16), cols[1].astype(BF16))
+    else:
+        lh, rh = column_halos(column(0, 0), column(1, w - 1))
     small = (top, bot, u, lh.astype(F32), rh.astype(F32), bias.reshape(1, c))
     block = pl.BlockSpec((n, w, c), lambda i: (i, 0, 0))
     return pl.pallas_call(

time: 29.8 us -> 32.5 us (1.091)
  starting transfers between devices: 5.06 us -> 9.02 us
  waiting for transfers between devices: 5.6 us -> 4.25 us
    ppermute x3 -> x5, starting transfers between devices: 5.06 us -> 9.02 us  [the longest x4 7.8 us: row_swap(): return lax.ppermute(x, axis, pairs + [(b, a) for a, b in pairs])]
    ppermute x3 -> x5, waiting for transfers between devices: 5.6 us -> 4.25 us  [the longest x4 4.25 us: row_swap(): return lax.ppermute(x, axis, pairs + [(b, a) for a, b in pairs])]
  transfers between devices with their start and end apart: 3 -> 5, of which waited for: 2 -> 1; matrix products, arithmetic and copies ran while one was open for 0% -> 1% of each run, Pallas kernels for 3% -> 3%
where the time goes in v7:
time: 32.5 us; the launch traced here: 32.3 us
  Pallas kernels  18.6 us (57%)
  starting transfers between devices  9.02 us (28%)
  waiting for transfers between devices  4.25 us (13%)
    pallas_call x1, Pallas kernels, on_device(): pl.pallas_call(conv_kernel, grid=(th // n,), out_shape=jax.ShapeDtypeStru...  16.2 us
    ppermute x4, starting transfers between devices, row_swap(): return lax.ppermute(x, axis, pairs + [(b, a) for a, b in pairs])  7.8 us
    ppermute x4, waiting for transfers between devices, row_swap(): return lax.ppermute(x, axis, pairs + [(b, a) for a, b in pairs])  4.25 us
    pallas_call x1, Pallas kernels, on_device(): pl.pallas_call(ends_kernel, grid=(1,), out_shape=ends, in_specs=[one_row(...  1.41 us
    ppermute x1, starting transfers between devices, columns_of_two(): mid = lax.ppermute(side, 'col', [(0, 1), (1, 0)])  1.23 us
    pallas_call x1, Pallas kernels, on_device(): pl.pallas_call(weights_kernel, grid=(1,), out_shape=weights, in_specs=[wh...  0.99 us
  transfers between devices with their start and end apart: 5, of which 1 were waited for; matrix products, arithmetic and copies ran while one was open for 1% of the time, Pallas kernels for 3%

profile of v7, /device:TPU:25, one launch (start us, length us, event | category | flops | bytes accessed | tf_op | source)
XLA Modules:
  0.0 32.3 jit_solution(9617624221419874912)
XLA Ops:
  0.0 0.0 copy-start.1
  0.0 0.0 copy-start.2
  0.0 0.0 copy-start.4
  0.0 0.0 copy-start
  0.0 1.4 %ends.1 = (bf16[2,256,256]{2,1,0:T(8,128)(2,1)S(1)}, f32[2,48,256]{2,1,0:T(8,128)S(1)}) custom-call(bf16[48,256,256]{2,1,0:T(8,128)(2,1)} %after.1, bf16[48,256,256]{2,1,0:T(8,128)(2,1)} %after.1, bf16[48,256,256]{2,1,0:T(8,128)(2,1)} %after.1, bf16[48,256,256]{2,1,0:T(8,128)(2,1)} %after.1), custom_call_target="tpu_custom_call" | custom-call | tf_op jit(solution)/shard_map/ends/pallas_call | solution.py:141
  1.5 1.9 %collective-permute-start.3 = (bf16[16,256]{1,0:T(8,128)(2,1)S(1)}, bf16[16,256]{1,0:T(8,128)(2,1)S(1)}, u32[]{:S(2)}, u32[]{:S(2)}) collective-permute-start(bf16[16,256]{1,0:T(8,128)(2,1)S(1)} %get-tuple-element.15), channel_id=1, source_target_pairs={{0,3},{1,2},{4,7},{5,6},{8,11},{9,10},{12,15},{13,14},{16,19},{17,... | collective-permute-start | bytes 24584 | tf_op jit(solution)/shard_map/ppermute | solution.py:95
  3.3 2.8 %collective-permute-start.2 = (bf16[16,256]{1,0:T(8,128)(2,1)S(1)}, bf16[16,256]{1,0:T(8,128)(2,1)S(1)}, u32[]{:S(2)}, u32[]{:S(2)}) collective-permute-start(bf16[16,256]{1,0:T(8,128)(2,1)S(1)} %get-tuple-element.16), channel_id=1, source_target_pairs={{2,5},{3,4},{6,9},{7,8},{10,13},{11,12},{14,17},{15,16},{18,21},{1... | collective-permute-start | bytes 24584 | tf_op jit(solution)/shard_map/ppermute | solution.py:95
  6.2 1.2 %collective-permute-start.4 = (bf16[48,256]{1,0:T(8,128)(2,1)S(1)}, bf16[48,256]{1,0:T(8,128)(2,1)S(1)}, u32[]{:S(2)}, u32[]{:S(2)}) collective-permute-start(bf16[48,256]{1,0:T(8,128)(2,1)S(1)} %fusion), channel_id=1, source_target_pairs={{0,1},{1,0},{2,3},{3,2},{4,5},{5,4},{6,7},{7,6},{8,9},{9,8},{10,11... | collective-permute-start | bytes 73736 | tf_op jit(solution)/shard_map/ppermute | solution.py:111
  7.5 0.9 %collective-permute-start.1 = (bf16[256,256]{1,0:T(8,128)(2,1)S(1)}, bf16[256,256]{1,0:T(8,128)(2,1)S(1)}, u32[]{:S(2)}, u32[]{:S(2)}) collective-permute-start(bf16[256,256]{1,0:T(8,128)(2,1)S(1)} %get-tuple-element.11), channel_id=1, source_target_pairs={{0,2},{4,6},{8,10},{12,14},{16,18},{20,22},{24,26},{28,30},{2,0},{... | collective-permute-start | bytes 393224 | tf_op jit(solution)/shard_map/ppermute | solution.py:95
  8.4 2.2 %collective-permute-start = (bf16[256,256]{1,0:T(8,128)(2,1)S(1)}, bf16[256,256]{1,0:T(8,128)(2,1)S(1)}, u32[]{:S(2)}, u32[]{:S(2)}) collective-permute-start(bf16[256,256]{1,0:T(8,128)(2,1)S(1)} %get-tuple-element.12), channel_id=1, source_target_pairs={{2,4},{6,8},{10,12},{14,16},{18,20},{22,24},{26,28},{4,2},{8,6},{1... | collective-permute-start | bytes 393224 | tf_op jit(solution)/shard_map/ppermute | solution.py:95
  10.6 0.0 copy-done.1
  10.6 0.0 copy-done.2
  10.6 0.0 copy-done.3
  10.6 0.0 copy-done.4
  10.6 1.0 %weights.1.u_ref = bf16[4,768,256]{2,1,0:T(8,128)(2,1)S(1)} custom-call(bf16[256,512]{1,0:T(8,128)(2,1)S(1)} %copy-done.1, f32[3,512]{1,0:T(4,128)S(1)} %copy-done.3, f32[3,512]{1,0:T(4,128)S(1)} %copy-done.4, bf16[512,256]{1,0:T(8,128)(2,1)S(1)} %copy-done.2), custom_call_target="tpu_custom_call" | custom-call | flops 805306368 | bytes 3145728 | tf_op jit(solution)/shard_map/weights/pallas_call | solution.py:155
  11.6 0.1 pad.3.clone
  11.7 0.0 collective-permute-done.3
  11.7 0.0 collective-permute-done.2
  11.7 0.0 collective-permute-done.4
  11.7 0.1 convert_select_fusion
  11.8 0.0 collective-permute-done.1
  11.8 4.2 %collective-permute-done = bf16[256,256]{1,0:T(8,128)(2,1)S(1)} collective-permute-done((bf16[256,256]{1,0:T(8,128)(2,1)S(1)}, bf16[256,256]{1,0:T(8,128)(2,1)S(1)}, u32[]{:S(2)}, u32[]{:S(2)}) %collective-permute-start) | collective-permute-done | bytes 131104 | tf_op jit(solution)/shard_map/ppermute | solution.py:95
  16.1 0.0 copy-done
  16.1 16.2 %conv.1 = bf16[48,256,256]{2,1,0:T(8,128)(2,1)} custom-call(bf16[48,256,256]{2,1,0:T(8,128)(2,1)} %after.1, bf16[48,256,256]{2,1,0:T(8,128)(2,1)} %after.1, bf16[48,256,256]{2,1,0:T(8,128)(2,1)} %after.1, bf16[256,256]{1,0:T(8,128)(2,1)S(1)} %get-tuple-element.10.top, bf16[256,256]{1,0:T(8,128)(2,1)S(1)} %get-tuple-element.9.bot, ...), custom_call_target="tpu_custom_call" | custom-call | tf_op jit(solution)/shard_map/conv/pallas_call | solution.py:179
  (9 shorter events, 0.1 us)
Async XLA Ops:
  0.0 10.6 %copy-start.1 = (bf16[256,512]{1,0:T(8,128)(2,1)S(1)}, bf16[256,512]{1,0:T(8,128)(2,1)}, u32[]{:S(2)}) copy-start(bf16[256,512]{1,0:T(8,128)(2,1)} %pin_ref.1) | copy-start | bytes 786436
  0.0 10.6 %copy-start.2 = (bf16[512,256]{1,0:T(8,128)(2,1)S(1)}, bf16[512,256]{1,0:T(8,128)(2,1)}, u32[]{:S(2)}) copy-start(bf16[512,256]{1,0:T(8,128)(2,1)} %po_ref.1) | copy-start | bytes 786436
  0.0 10.6 %copy-start.3 = (f32[3,512]{1,0:T(4,128)S(1)}, f32[3,512]{1,0:T(4,128)}, u32[]{:S(2)}) copy-start(f32[3,512]{1,0:T(4,128)} %tw_ref.1) | copy-start | bytes 18436
  0.0 10.6 %copy-start.4 = (f32[3,512]{1,0:T(4,128)S(1)}, f32[3,512]{1,0:T(4,128)}, u32[]{:S(2)}) copy-start(f32[3,512]{1,0:T(4,128)} %tt_ref.1) | copy-start | bytes 18436
  0.0 16.1 %copy-start = (f32[256]{0:T(256)S(1)}, f32[256]{0:T(256)}, u32[]{:S(2)}) copy-start(f32[256]{0:T(256)} %param.11) | copy-start | bytes 3076
  1.5 10.2 %collective-permute-start.3 = (bf16[16,256]{1,0:T(8,128)(2,1)S(1)}, bf16[16,256]{1,0:T(8,128)(2,1)S(1)}, u32[]{:S(2)}, u32[]{:S(2)}) collective-permute-start(bf16[16,256]{1,0:T(8,128)(2,1)S(1)} %get-tuple-element.15), channel_id=1, source_target_pairs={{0,3},{1,2},{4,7},{5,6},{8,11},{9,10},{12,15},{13,14},{16,19},{17,... | collective-permute-start | bytes 24584 | tf_op jit(solution)/shard_map/ppermute | solution.py:95
  3.3 8.3 %collective-permute-start.2 = (bf16[16,256]{1,0:T(8,128)(2,1)S(1)}, bf16[16,256]{1,0:T(8,128)(2,1)S(1)}, u32[]{:S(2)}, u32[]{:S(2)}) collective-permute-start(bf16[16,256]{1,0:T(8,128)(2,1)S(1)} %get-tuple-element.16), channel_id=1, source_target_pairs={{2,5},{3,4},{6,9},{7,8},{10,13},{11,12},{14,17},{15,16},{18,21},{1... | collective-permute-start | bytes 24584 | tf_op jit(solution)/shard_map/ppermute | solution.py:95
  6.2 5.5 %collective-permute-start.4 = (bf16[48,256]{1,0:T(8,128)(2,1)S(1)}, bf16[48,256]{1,0:T(8,128)(2,1)S(1)}, u32[]{:S(2)}, u32[]{:S(2)}) collective-permute-start(bf16[48,256]{1,0:T(8,128)(2,1)S(1)} %fusion), channel_id=1, source_target_pairs={{0,1},{1,0},{2,3},{3,2},{4,5},{5,4},{6,7},{7,6},{8,9},{9,8},{10,11... | collective-permute-start | bytes 73736 | tf_op jit(solution)/shard_map/ppermute | solution.py:111
  7.5 4.3 %collective-permute-start.1 = (bf16[256,256]{1,0:T(8,128)(2,1)S(1)}, bf16[256,256]{1,0:T(8,128)(2,1)S(1)}, u32[]{:S(2)}, u32[]{:S(2)}) collective-permute-start(bf16[256,256]{1,0:T(8,128)(2,1)S(1)} %get-tuple-element.11), channel_id=1, source_target_pairs={{0,2},{4,6},{8,10},{12,14},{16,18},{20,22},{24,26},{28,30},{2,0},{... | collective-permute-start | bytes 393224 | tf_op jit(solution)/shard_map/ppermute | solution.py:95
  8.4 7.7 %collective-permute-start = (bf16[256,256]{1,0:T(8,128)(2,1)S(1)}, bf16[256,256]{1,0:T(8,128)(2,1)S(1)}, u32[]{:S(2)}, u32[]{:S(2)}) collective-permute-start(bf16[256,256]{1,0:T(8,128)(2,1)S(1)} %get-tuple-element.12), channel_id=1, source_target_pairs={{2,4},{6,8},{10,12},{14,16},{18,20},{22,24},{26,28},{4,2},{8,6},{1... | collective-permute-start | bytes 393224 | tf_op jit(solution)/shard_map/ppermute | solution.py:95

commit v8 on v6

--- a/solution.py
+++ b/solution.py
@@ -19,7 +19,7 @@
     foot = jnp.where(at == 15, tail, right[w - 16 :].astype(F32)).astype(BF16)
     left = jnp.concatenate([head, left[16:]], axis=0)
     right = jnp.concatenate([right[: w - 16], foot], axis=0)
-    return jnp.concatenate([left, x, right], axis=1)
+    return left, x, right
 
 
 def conv_kernel(before, here, after, top, bot, u_ref, lh_ref, rh_ref, bias_ref, out_ref,
@@ -39,7 +39,12 @@
             both(ref[pl.ds(i * n + a, 1), :], ref[pl.ds(i * n + b, 1), :]) for ref in (lh_ref, rh_ref)
         ]
         lhs = with_sides(both(centre(a), centre(b)), lead, tail)
-        return jnp.dot(lhs, u_ref[k], preferred_element_type=F32)
+        c = u_ref.shape[2]
+        parts = [
+            jnp.dot(x, u_ref[k, j * c : (j + 1) * c, :], preferred_element_type=F32)
+            for j, x in enumerate(lhs)
+        ]
+        return parts[0] + parts[1] + parts[2]
 
     def finish(r, half):
         x = here[r].astype(F32)
@@ -56,9 +61,12 @@
         finish(r + 1, (m1 - m2) - m3 + bias)
 
 
-def ends_kernel(first, last, left, right, rows_ref, cols_ref):
+def rows_kernel(first, last, rows_ref):
     rows_ref[0] = first[0]
     rows_ref[1] = last[0]
+
+
+def columns_kernel(left, right, cols_ref):
     for r in range(left.shape[0]):
         cols_ref[0, r : r + 1, :] = left[r].astype(F32)[:1]
         cols_ref[1, r : r + 1, :] = right[r].astype(F32)[-1:]
@@ -123,18 +131,29 @@
         return pl.BlockSpec((th, 16, c), lambda i: (0, at, 0))
 
     params = pltpu.CompilerParams(vmem_limit_bytes=48 * MIB)
-    ends = jax.ShapeDtypeStruct((2, w, c), BF16), jax.ShapeDtypeStruct((2, th, c), F32)
-    rows, cols = pl.pallas_call(
-        ends_kernel,
+    rows = jax.ShapeDtypeStruct((2, w, c), BF16)
+    rows = pl.pallas_call(
+        rows_kernel,
         grid=(1,),
-        out_shape=ends,
-        in_specs=[one_row(lambda i: 0), one_row(lambda i: th - 1),
-                  some_columns(0), some_columns(w // 16 - 1)],
-        out_specs=tuple(whole(x) for x in ends),
-        compiler_params=params,
-        name="ends",
-    )(image, image, image, image)
+        out_shape=rows,
+        in_specs=[one_row(lambda i: 0), one_row(lambda i: th - 1)],
+        out_specs=whole(rows),
+        compiler_params=params,
+        name="rows",
+    )(image, image)
     top, bot = row_halos(rows[0], rows[1])
+
+    cols = jax.ShapeDtypeStruct((2, th, c), F32)
+    cols = pl.pallas_call(
+        columns_kernel,
+        grid=(1,),
+        out_shape=cols,
+        in_specs=[some_columns(0), some_columns(w // 16 - 1)],
+        out_specs=whole(cols),
+        compiler_params=params,
+        cost_estimate=pl.CostEstimate(flops=0, bytes_accessed=3 * MIB, transcendentals=0),
+        name="columns",
+    )(image, image)
 
     args = (proj_in, taps_wide, taps_tall, proj_out)
     weights = jax.ShapeDtypeStruct((4, 3 * c, c), BF16)

time: 29.8 us -> 29.9 us (level)
  waiting for transfers between devices: 5.6 us -> 4.27 us
  Pallas kernels: 18.6 us -> 19.9 us
    ppermute x2, waiting for transfers between devices: 4.54 us -> 3.22 us  [swap(): return lax.ppermute(x, 'row', pairs + [(b, a) for a, b in pairs])]
    pallas_call x1 -> x2, Pallas kernels: 1.41 us -> 2.25 us  [the longest x1 1.26 us: on_device(): pl.pallas_call(columns_kernel, grid=(1,), out_shape=cols, in_specs=[some_...]
    pallas_call x1, Pallas kernels: 16.2 us -> 16.7 us  [on_device(): pl.pallas_call(conv_kernel, grid=(th // n,), out_shape=jax.ShapeDtypeStru...]
  transfers between devices with their start and end apart: 3 -> 3, of which waited for: 2 -> 2; matrix products, arithmetic and copies ran while one was open for 0% -> 0% of each run, Pallas kernels for 3% -> 8%
where the time goes in v8:
time: 29.9 us; the launch traced here: 29.7 us
  Pallas kernels  19.9 us (67%)
  starting transfers between devices  5.06 us (17%)
  waiting for transfers between devices  4.27 us (14%)
    pallas_call x1, Pallas kernels, on_device(): pl.pallas_call(conv_kernel, grid=(th // n,), out_shape=jax.ShapeDtypeStru...  16.7 us
    ppermute x2, starting transfers between devices, swap(): return lax.ppermute(x, 'row', pairs + [(b, a) for a, b in pairs])  3.76 us
    ppermute x2, waiting for transfers between devices, swap(): return lax.ppermute(x, 'row', pairs + [(b, a) for a, b in pairs])  3.22 us
    ppermute x1, starting transfers between devices, column_halos(): got = lax.ppermute(jnp.where(low, last, first), 'col', [(0, 1), (1, 0)])  1.3 us
    pallas_call x1, Pallas kernels, on_device(): pl.pallas_call(columns_kernel, grid=(1,), out_shape=cols, in_specs=[some_...  1.26 us
    ppermute x1, waiting for transfers between devices, column_halos(): got = lax.ppermute(jnp.where(low, last, first), 'col', [(0, 1), (1, 0)])  1.06 us
    pallas_call x1, Pallas kernels, on_device(): pl.pallas_call(weights_kernel, grid=(1,), out_shape=weights, in_specs=[wh...  1 us
    pallas_call x1, Pallas kernels, on_device(): pl.pallas_call(rows_kernel, grid=(1,), out_shape=rows, in_specs=[one_row(...  0.98 us
  transfers between devices with their start and end apart: 3, of which 2 were waited for; matrix products, arithmetic and copies ran while one was open for 0% of the time, Pallas kernels for 8%

profile of v8, /device:TPU:25, one launch (start us, length us, event | category | flops | bytes accessed | tf_op | source)
XLA Modules:
  0.0 29.7 jit_solution(14668143107010766207)
XLA Ops:
  0.0 1.0 %rows.1 = bf16[2,256,256]{2,1,0:T(8,128)(2,1)S(1)} custom-call(bf16[48,256,256]{2,1,0:T(8,128)(2,1)} %after.1, bf16[48,256,256]{2,1,0:T(8,128)(2,1)} %after.1), custom_call_target="tpu_custom_call" | custom-call | tf_op jit(solution)/shard_map/rows/pallas_call | solution.py:135
  1.0 0.7 %collective-permute-start.1 = (bf16[256,256]{1,0:T(8,128)(2,1)S(1)}, bf16[256,256]{1,0:T(8,128)(2,1)S(1)}, u32[]{:S(2)}, u32[]{:S(2)}) collective-permute-start(bf16[256,256]{1,0:T(8,128)(2,1)S(1)} %get-tuple-element.7), channel_id=1, source_target_pairs={{0,2},{4,6},{8,10},{12,14},{16,18},{20,22},{24,26},{28,30},{2,0},{... | collective-permute-start | bytes 393224 | tf_op jit(solution)/shard_map/ppermute | solution.py:104
  1.8 3.0 %collective-permute-start = (bf16[256,256]{1,0:T(8,128)(2,1)S(1)}, bf16[256,256]{1,0:T(8,128)(2,1)S(1)}, u32[]{:S(2)}, u32[]{:S(2)}) collective-permute-start(bf16[256,256]{1,0:T(8,128)(2,1)S(1)} %get-tuple-element.8), channel_id=1, source_target_pairs={{2,4},{6,8},{10,12},{14,16},{18,20},{22,24},{26,28},{4,2},{8,6},{1... | collective-permute-start | bytes 393224 | tf_op jit(solution)/shard_map/ppermute | solution.py:104
  4.8 0.0 copy-start.1
  4.8 0.0 copy-start.2
  4.8 0.0 copy-start.3
  4.8 0.0 copy-start.4
  4.8 0.0 copy-start
  4.8 1.3 %columns.1 = f32[2,48,256]{2,1,0:T(8,128)S(1)} custom-call(bf16[48,256,256]{2,1,0:T(8,128)(2,1)} %after.1, bf16[48,256,256]{2,1,0:T(8,128)(2,1)} %after.1), custom_call_target="tpu_custom_call" | custom-call | bytes 3145728 | tf_op jit(solution)/shard_map/columns/pallas_call | solution.py:147
  6.1 0.1 pad.7.clone
  6.2 0.0 collective-permute-done.1
  6.2 3.2 %collective-permute-done = bf16[256,256]{1,0:T(8,128)(2,1)S(1)} collective-permute-done((bf16[256,256]{1,0:T(8,128)(2,1)S(1)}, bf16[256,256]{1,0:T(8,128)(2,1)S(1)}, u32[]{:S(2)}, u32[]{:S(2)}) %collective-permute-start) | collective-permute-done | bytes 131104 | tf_op jit(solution)/shard_map/ppermute | solution.py:104
  9.5 0.1 maximum_select_fusion
  9.6 1.3 %collective-permute-start.2 = (bf16[64,256]{1,0:T(8,128)(2,1)S(1)}, bf16[64,256]{1,0:T(8,128)(2,1)S(1)}, u32[]{:S(2)}, u32[]{:S(2)}) collective-permute-start(bf16[64,256]{1,0:T(8,128)(2,1)S(1)} %maximum_select_fusion), channel_id=1, source_target_pairs={{0,1},{1,0},{2,3},{3,2},{4,5},{5,4},{6,7},{7,6},{8,9},{9,8},{10,11... | collective-permute-start | bytes 98312 | tf_op jit(solution)/shard_map/ppermute | solution.py:114
  10.9 0.0 copy-done.1
  10.9 0.0 copy-done.2
  10.9 0.0 copy-done.3
  10.9 0.0 copy-done.4
  10.9 1.0 %weights.1.u_ref = bf16[4,768,256]{2,1,0:T(8,128)(2,1)S(1)} custom-call(bf16[256,512]{1,0:T(8,128)(2,1)S(1)} %copy-done.1, f32[3,512]{1,0:T(4,128)S(1)} %copy-done.3, f32[3,512]{1,0:T(4,128)S(1)} %copy-done.4, bf16[512,256]{1,0:T(8,128)(2,1)S(1)} %copy-done.2), custom_call_target="tpu_custom_call" | custom-call | flops 805306368 | bytes 3145728 | tf_op jit(solution)/shard_map/weights/pallas_call | solution.py:160
  11.9 1.1 %collective-permute-done.2 = bf16[64,256]{1,0:T(8,128)(2,1)S(1)} collective-permute-done((bf16[64,256]{1,0:T(8,128)(2,1)S(1)}, bf16[64,256]{1,0:T(8,128)(2,1)S(1)}, u32[]{:S(2)}, u32[]{:S(2)}) %collective-permute-start.2) | collective-permute-done | bytes 32800 | tf_op jit(solution)/shard_map/ppermute | solution.py:114
  13.0 0.0 copy-done
  13.0 16.7 %conv.1 = bf16[48,256,256]{2,1,0:T(8,128)(2,1)} custom-call(bf16[48,256,256]{2,1,0:T(8,128)(2,1)} %after.1, bf16[48,256,256]{2,1,0:T(8,128)(2,1)} %after.1, bf16[48,256,256]{2,1,0:T(8,128)(2,1)} %after.1, bf16[256,256]{1,0:T(8,128)(2,1)S(1)} %get-tuple-element.6.top, bf16[256,256]{1,0:T(8,128)(2,1)S(1)} %get-tuple-element.5.bot, ...), custom_call_target="tpu_custom_call" | custom-call | tf_op jit(solution)/shard_map/conv/pallas_call | solution.py:181
  (7 shorter events, 0.1 us)
Async XLA Ops:
  1.0 5.2 %collective-permute-start.1 = (bf16[256,256]{1,0:T(8,128)(2,1)S(1)}, bf16[256,256]{1,0:T(8,128)(2,1)S(1)}, u32[]{:S(2)}, u32[]{:S(2)}) collective-permute-start(bf16[256,256]{1,0:T(8,128)(2,1)S(1)} %get-tuple-element.7), channel_id=1, source_target_pairs={{0,2},{4,6},{8,10},{12,14},{16,18},{20,22},{24,26},{28,30},{2,0},{... | collective-permute-start | bytes 393224 | tf_op jit(solution)/shard_map/ppermute | solution.py:104
  1.8 7.7 %collective-permute-start = (bf16[256,256]{1,0:T(8,128)(2,1)S(1)}, bf16[256,256]{1,0:T(8,128)(2,1)S(1)}, u32[]{:S(2)}, u32[]{:S(2)}) collective-permute-start(bf16[256,256]{1,0:T(8,128)(2,1)S(1)} %get-tuple-element.8), channel_id=1, source_target_pairs={{2,4},{6,8},{10,12},{14,16},{18,20},{22,24},{26,28},{4,2},{8,6},{1... | collective-permute-start | bytes 393224 | tf_op jit(solution)/shard_map/ppermute | solution.py:104
  4.8 6.1 %copy-start.1 = (bf16[256,512]{1,0:T(8,128)(2,1)S(1)}, bf16[256,512]{1,0:T(8,128)(2,1)}, u32[]{:S(2)}) copy-start(bf16[256,512]{1,0:T(8,128)(2,1)} %pin_ref.1) | copy-start | bytes 786436
  4.8 6.1 %copy-start.2 = (bf16[512,256]{1,0:T(8,128)(2,1)S(1)}, bf16[512,256]{1,0:T(8,128)(2,1)}, u32[]{:S(2)}) copy-start(bf16[512,256]{1,0:T(8,128)(2,1)} %po_ref.1) | copy-start | bytes 786436
  4.8 6.1 %copy-start.3 = (f32[3,512]{1,0:T(4,128)S(1)}, f32[3,512]{1,0:T(4,128)}, u32[]{:S(2)}) copy-start(f32[3,512]{1,0:T(4,128)} %tw_ref.1) | copy-start | bytes 18436
  4.8 6.1 %copy-start.4 = (f32[3,512]{1,0:T(4,128)S(1)}, f32[3,512]{1,0:T(4,128)}, u32[]{:S(2)}) copy-start(f32[3,512]{1,0:T(4,128)} %tt_ref.1) | copy-start | bytes 18436
  4.8 8.1 %copy-start = (f32[256]{0:T(256)S(1)}, f32[256]{0:T(256)}, u32[]{:S(2)}) copy-start(f32[256]{0:T(256)} %param.11) | copy-start | bytes 3076
  9.6 3.4 %collective-permute-start.2 = (bf16[64,256]{1,0:T(8,128)(2,1)S(1)}, bf16[64,256]{1,0:T(8,128)(2,1)S(1)}, u32[]{:S(2)}, u32[]{:S(2)}) collective-permute-start(bf16[64,256]{1,0:T(8,128)(2,1)S(1)} %maximum_select_fusion), channel_id=1, source_target_pairs={{0,1},{1,0},{2,3},{3,2},{4,5},{5,4},{6,7},{7,6},{8,9},{9,8},{10,11... | collective-permute-start | bytes 98312 | tf_op jit(solution)/shard_map/ppermute | solution.py:114

commit v9 on v8

--- a/solution.py
+++ b/solution.py
@@ -8,7 +8,7 @@
 BF16 = jnp.bfloat16
 F32 = jnp.float32
 MIB = 1 << 20
-ROWS = 8
+ROWS = 4
 
 
 def with_sides(x, lead, tail):
@@ -19,46 +19,56 @@
     foot = jnp.where(at == 15, tail, right[w - 16 :].astype(F32)).astype(BF16)
     left = jnp.concatenate([head, left[16:]], axis=0)
     right = jnp.concatenate([right[: w - 16], foot], axis=0)
-    return left, x, right
-
-
-def conv_kernel(before, here, after, top, bot, u_ref, lh_ref, rh_ref, bias_ref, out_ref,
-                ends):
-    i = pl.program_id(0)
-    n, w, _ = here.shape
+    return jnp.concatenate([left, x, right], axis=1)
+
+
+def write_block(here, centre, base, u_ref, lh_ref, rh_ref, bias_ref, out_ref):
     bias = bias_ref[...] * 0.5
-
-    def centre(r):
-        return here[r - 1] if 0 < r <= n else ends[r // n]
 
     def product(k, a, b, add):
         def both(x, y):
             return x + y if add else x - y
 
         lead, tail = [
-            both(ref[pl.ds(i * n + a, 1), :], ref[pl.ds(i * n + b, 1), :]) for ref in (lh_ref, rh_ref)
+            both(ref[pl.ds(base + a, 1), :], ref[pl.ds(base + b, 1), :]) for ref in (lh_ref, rh_ref)
         ]
         lhs = with_sides(both(centre(a), centre(b)), lead, tail)
-        c = u_ref.shape[2]
-        parts = [
-            jnp.dot(x, u_ref[k, j * c : (j + 1) * c, :], preferred_element_type=F32)
-            for j, x in enumerate(lhs)
-        ]
-        return parts[0] + parts[1] + parts[2]
+        return jnp.dot(lhs, u_ref[k], preferred_element_type=F32)
 
     def finish(r, half):
         x = here[r].astype(F32)
         out_ref[r] = (x + (half + half * jnp.tanh(half))).astype(BF16)
 
-    ends[0] = jnp.where(i == 0, top[...], before[0])
-    ends[1] = jnp.where(i == pl.num_programs(0) - 1, bot[...], after[0])
-    for r in range(0, n, 2):
+    for r in range(0, here.shape[0], 2):
         m1 = product(1, r + 1, r + 2, True)
         m2 = product(2, r + 2, r + 1, False)
         m0 = product(0, r, r + 2, False)
         m3 = product(3, r + 1, r + 3, False)
         finish(r, m0 + (m1 + m2) + bias)
         finish(r + 1, (m1 - m2) - m3 + bias)
+
+
+def inner_kernel(before, here, after, u_ref, lh_ref, rh_ref, bias_ref, out_ref):
+    n = here.shape[0]
+
+    def centre(r):
+        return before[0] if r == 0 else after[0] if r > n else here[r - 1]
+
+    base = (pl.program_id(0) + 1) * n - 1
+    write_block(here, centre, base, u_ref, lh_ref, rh_ref, bias_ref, out_ref)
+
+
+def edge_kernel(here, second, top, bot, u_ref, lh_ref, rh_ref, bias_ref, out_ref, ends):
+    i = pl.program_id(0)
+    n, w, _ = here.shape
+    ends[0] = jnp.where(i == 0, top[0:w, :], second[0])
+    ends[1] = jnp.where(i == 0, second[0], bot[0:w, :])
+
+    def centre(r):
+        return here[r - 1] if 0 < r <= n else ends[r // n]
+
+    base = i * (lh_ref.shape[0] - 16 - n)
+    write_block(here, centre, base, u_ref, lh_ref, rh_ref, bias_ref, out_ref)
 
 
 def rows_kernel(first, last, rows_ref):
@@ -131,6 +141,18 @@
         return pl.BlockSpec((th, 16, c), lambda i: (0, at, 0))
 
     params = pltpu.CompilerParams(vmem_limit_bytes=48 * MIB)
+    cols = jax.ShapeDtypeStruct((2, th, c), F32)
+    cols = pl.pallas_call(
+        columns_kernel,
+        grid=(1,),
+        out_shape=cols,
+        in_specs=[some_columns(0), some_columns(w // 16 - 1)],
+        out_specs=whole(cols),
+        compiler_params=params,
+        cost_estimate=pl.CostEstimate(flops=0, bytes_accessed=3 * MIB, transcendentals=0),
+        name="columns",
+    )(image, image)
+
     rows = jax.ShapeDtypeStruct((2, w, c), BF16)
     rows = pl.pallas_call(
         rows_kernel,
@@ -139,21 +161,16 @@
         in_specs=[one_row(lambda i: 0), one_row(lambda i: th - 1)],
         out_specs=whole(rows),
         compiler_params=params,
+        cost_estimate=pl.CostEstimate(flops=0, bytes_accessed=3 * MIB, transcendentals=0),
         name="rows",
     )(image, image)
-    top, bot = row_halos(rows[0], rows[1])
-
-    cols = jax.ShapeDtypeStruct((2, th, c), F32)
-    cols = pl.pallas_call(
-        columns_kernel,
-        grid=(1,),
-        out_shape=cols,
-        in_specs=[some_columns(0), some_columns(w // 16 - 1)],
-        out_specs=whole(cols),
-        compiler_params=params,
-        cost_estimate=pl.CostEstimate(flops=0, bytes_accessed=3 * MIB, transcendentals=0),
-        name="columns",
-    )(image, image)
+    lh, rh = column_halos(cols[0].astype(BF16), cols[1].astype(BF16))
+
+    def extended(k, at):
+        pad = jnp.zeros((14, c), BF16)
+        return jnp.concatenate([rows[k], lh[at][None], rh[at][None], pad], axis=0)
+
+    top, bot = row_halos(extended(0, 0), extended(1, th - 1))
 
     args = (proj_in, taps_wide, taps_tall, proj_out)
     weights = jax.ShapeDtypeStruct((4, 3 * c, c), BF16)
@@ -170,29 +187,51 @@
         name="weights",
     )(*args)
 
-    def column(k, at):
+    def column(x, at):
         pad = jnp.zeros((14, c), BF16)
-        return jnp.concatenate(
-            [top[at][None], cols[k].astype(BF16), bot[at][None], pad], axis=0)
-
-    lh, rh = column_halos(column(0, 0), column(1, w - 1))
-    small = (top, bot, u, lh.astype(F32), rh.astype(F32), bias.reshape(1, c))
-    block = pl.BlockSpec((n, w, c), lambda i: (i, 0, 0))
-    return pl.pallas_call(
-        conv_kernel,
-        grid=(th // n,),
+        return jnp.concatenate([top[at][None], x, bot[at][None], pad], axis=0).astype(F32)
+
+    def cost(count):
+        return pl.CostEstimate(
+            flops=count * 12 * w * c * c, bytes_accessed=4 * count * w * c,
+            transcendentals=count * w * c)
+
+    bias2 = bias.reshape(1, c)
+    small = (u, lh.astype(F32), rh.astype(F32), bias2)
+    inner = pl.pallas_call(
+        inner_kernel,
+        grid=(th // n - 2,),
         out_shape=jax.ShapeDtypeStruct(image.shape, BF16),
         in_specs=[
-            one_row(lambda i: jnp.maximum(i * n - 1, 0)),
-            block,
-            one_row(lambda i: jnp.minimum(i * n + n, th - 1)),
+            one_row(lambda i: (i + 1) * n - 1),
+            pl.BlockSpec((n, w, c), lambda i: (i + 1, 0, 0)),
+            one_row(lambda i: (i + 2) * n),
             *[whole(x) for x in small],
         ],
-        out_specs=block,
+        out_specs=pl.BlockSpec((n, w, c), lambda i: (i + 1, 0, 0)),
+        compiler_params=params,
+        cost_estimate=cost(th - 2 * n),
+        name="inner",
+    )(image, image, image, *small)
+
+    small = (top, bot, u, column(lh, w), column(rh, w + 1), bias2)
+    edges = pl.pallas_call(
+        edge_kernel,
+        grid=(2,),
+        out_shape=jax.ShapeDtypeStruct((2 * n, w, c), BF16),
+        in_specs=[
+            pl.BlockSpec((n, w, c), lambda i: (i * (th // n - 1), 0, 0)),
+            one_row(lambda i: n + i * (th - 2 * n - 1)),
+            *[whole(x) for x in small],
+        ],
+        out_specs=pl.BlockSpec((n, w, c), lambda i: (i, 0, 0)),
         scratch_shapes=[pltpu.VMEM((2, w, c), BF16)],
         compiler_params=params,
-        name="conv",
-    )(image, image, image, *small)
+        cost_estimate=cost(2 * n),
+        name="edges",
+    )(image, image, *small)
+    out = lax.dynamic_update_slice(inner, edges[:n], (0, 0, 0))
+    return lax.dynamic_update_slice(out, edges[n:], (th - n, 0, 0))
 
 
 def solution(mesh):

time: 29.9 us -> 29.8 us (level)
  the two profiles are of different devices: /device:TPU:25 before, /device:TPU:1 now
where the time goes in v9:
time: 29.8 us; the launch traced here: 29.3 us
  Pallas kernels  20.8 us (70%)
  starting transfers between devices  6.4 us (21%)
  local copies, waits for them, and re-layouts  1.74 us (6%)
    pallas_call x1, Pallas kernels, on_device(): pl.pallas_call(inner_kernel, grid=(th // n - 2,), out_shape=jax.ShapeDtyp...  14.2 us
    ppermute x2, starting transfers between devices, swap(): return lax.ppermute(x, 'row', pairs + [(b, a) for a, b in pairs])  4.27 us
    pallas_call x1, Pallas kernels, on_device(): pl.pallas_call(edge_kernel, grid=(2,), out_shape=jax.ShapeDtypeStruct((2...  3.45 us
    ppermute x1, starting transfers between devices, column_halos(): got = lax.ppermute(jnp.where(low, last, first), 'col', [(0, 1), (1, 0)])  2.13 us
    pallas_call x1, Pallas kernels, on_device(): pl.pallas_call(columns_kernel, grid=(1,), out_shape=cols, in_specs=[some_...  1.21 us
    pallas_call x1, Pallas kernels, on_device(): pl.pallas_call(weights_kernel, grid=(1,), out_shape=weights, in_specs=[wh...  0.99 us
    pallas_call x1, Pallas kernels, on_device(): pl.pallas_call(rows_kernel, grid=(1,), out_shape=rows, in_specs=[one_row(...  0.98 us
    dynamic_update_slice x1, local copies, waits for them, and re-layouts, on_device(): out = lax.dynamic_update_slice(inner, edges[:n], (0, 0, 0))  0.83 us
  transfers between devices with their start and end apart: 3, of which 0 were waited for; matrix products, arithmetic and copies ran while one was open for 0% of the time, Pallas kernels for 55%

profile of v9, /device:TPU:1, one launch (start us, length us, event | category | flops | bytes accessed | tf_op | source)
XLA Modules:
  0.0 29.3 jit_solution(13865410130900580322)
XLA Ops:
  0.0 1.2 %columns.1 = f32[2,48,256]{2,1,0:T(8,128)S(1)} custom-call(bf16[48,256,256]{2,1,0:T(8,128)(2,1)} %second.1, bf16[48,256,256]{2,1,0:T(8,128)(2,1)} %second.1), custom_call_target="tpu_custom_call" | custom-call | bytes 3145728 | tf_op jit(solution)/shard_map/columns/pallas_call | solution.py:145
  1.2 0.0 copy-start.1
  1.3 0.0 copy-start.2
  1.3 0.0 copy-start.3
  1.3 0.0 copy-start.4
  1.3 0.0 copy-start
  1.3 2.1 %collective-permute-start = (bf16[48,256]{1,0:T(8,128)(2,1)S(1)}, bf16[48,256]{1,0:T(8,128)(2,1)S(1)}, u32[]{:S(2)}, u32[]{:S(2)}) collective-permute-start(bf16[48,256]{1,0:T(8,128)(2,1)S(1)} %fusion.2), channel_id=1, source_target_pairs={{0,1},{1,0},{2,3},{3,2},{4,5},{5,4},{6,7},{7,6},{8,9},{9,8},{10,11... | collective-permute-start | bytes 73736 | tf_op jit(solution)/shard_map/ppermute | solution.py:124
  3.4 1.0 %rows.1 = bf16[2,256,256]{2,1,0:T(8,128)(2,1)S(1)} custom-call(bf16[48,256,256]{2,1,0:T(8,128)(2,1)} %second.1, bf16[48,256,256]{2,1,0:T(8,128)(2,1)} %second.1), custom_call_target="tpu_custom_call" | custom-call | bytes 3145728 | tf_op jit(solution)/shard_map/rows/pallas_call | solution.py:157
  4.5 0.0 copy-done.1
  4.5 0.0 copy-done.2
  4.5 0.0 copy-done.3
  4.5 0.0 copy-done.4
  4.5 1.0 %weights.1.u_ref = bf16[4,768,256]{2,1,0:T(8,128)(2,1)S(1)} custom-call(bf16[256,512]{1,0:T(8,128)(2,1)S(1)} %copy-done.1, f32[3,512]{1,0:T(4,128)S(1)} %copy-done.3, f32[3,512]{1,0:T(4,128)S(1)} %copy-done.4, bf16[512,256]{1,0:T(8,128)(2,1)S(1)} %copy-done.2), custom_call_target="tpu_custom_call" | custom-call | flops 805306368 | bytes 3145728 | tf_op jit(solution)/shard_map/weights/pallas_call | solution.py:177
  5.5 0.0 collective-permute-done
  5.6 0.1 broadcast_select_fusion.2
  5.6 1.0 %collective-permute-start.2 = (bf16[272,256]{1,0:T(8,128)(2,1)S(1)}, bf16[272,256]{1,0:T(8,128)(2,1)S(1)}, u32[]{:S(2)}, u32[]{:S(2)}) collective-permute-start(bf16[272,256]{1,0:T(8,128)(2,1)S(1)} %get-tuple-element.11), channel_id=1, source_target_pairs={{0,2},{4,6},{8,10},{12,14},{16,18},{20,22},{24,26},{28,30},{2,0},{... | collective-permute-start | bytes 417800 | tf_op jit(solution)/shard_map/ppermute | solution.py:114
  6.7 3.2 %collective-permute-start.1 = (bf16[272,256]{1,0:T(8,128)(2,1)S(1)}, bf16[272,256]{1,0:T(8,128)(2,1)S(1)}, u32[]{:S(2)}, u32[]{:S(2)}) collective-permute-start(bf16[272,256]{1,0:T(8,128)(2,1)S(1)} %get-tuple-element.12), channel_id=1, source_target_pairs={{2,4},{6,8},{10,12},{14,16},{18,20},{22,24},{26,28},{4,2},{8,6},{1... | collective-permute-start | bytes 417800 | tf_op jit(solution)/shard_map/ppermute | solution.py:114
  9.9 0.0 copy-done
  9.9 14.2 %inner.1 = bf16[48,256,256]{2,1,0:T(8,128)(2,1)} custom-call(bf16[48,256,256]{2,1,0:T(8,128)(2,1)} %second.1, bf16[48,256,256]{2,1,0:T(8,128)(2,1)} %second.1, bf16[48,256,256]{2,1,0:T(8,128)(2,1)} %second.1, bf16[4,768,256]{2,1,0:T(8,128)(2,1)S(1)} %weights.1.u_ref, f32[48,256]{1,0:T(8,128)S(1)} %get-tuple-element.23.lh_ref, ...), custom_call_target="tpu_custom_call" | custom-call | flops 8053063680 | bytes 10485760 | tf_op jit(solution)/shard_map/inner/pallas_call | solution.py:201
  24.1 0.0 collective-permute-done.2
  24.1 0.0 collective-permute-done.1
  24.2 3.5 %edges.1 = bf16[8,256,256]{2,1,0:T(8,128)(2,1)S(1)} custom-call(bf16[48,256,256]{2,1,0:T(8,128)(2,1)} %second.1, bf16[48,256,256]{2,1,0:T(8,128)(2,1)} %second.1, bf16[272,256]{1,0:T(8,128)(2,1)S(1)} %get-tuple-element.10.top, bf16[272,256]{1,0:T(8,128)(2,1)S(1)} %get-tuple-element.9.bot, bf16[4,768,256]{2,1,0:T(8,128)(2,1)S(1)} %weights.1.u_ref, ...), custom_call_target="tpu_custom_call" | custom-call | flops 1610612736 | bytes 2097152 | tf_op jit(solution)/shard_map/edges/pallas_call | solution.py:218
  27.6 0.8 %slice_dynamic-update-slice_fusion.1 = bf16[48,256,256]{2,1,0:T(8,128)(2,1)} fusion(bf16[48,256,256]{2,1,0:T(8,128)(2,1)} %inner.1, bf16[8,256,256]{2,1,0:T(8,128)(2,1)S(1)} %edges.1), kind=kLoop, calls=%fused_computation.1 | loop fusion | bytes 1048576 | tf_op jit(solution)/shard_map/dynamic_update_slice | solution.py:233
  28.5 0.8 %slice_dynamic-update-slice_fusion = bf16[48,256,256]{2,1,0:T(8,128)(2,1)} fusion(bf16[48,256,256]{2,1,0:T(8,128)(2,1)} %slice_dynamic-update-slice_fusion.1, bf16[8,256,256]{2,1,0:T(8,128)(2,1)S(1)} %edges.1), kind=kLoop, calls=%fused_computation | loop fusion | bytes 1048576 | tf_op jit(solution)/shard_map/dynamic_update_slice | solution.py:234
  (10 shorter events, 0.1 us)
Async XLA Ops:
  1.2 3.2 %copy-start.1 = (bf16[256,512]{1,0:T(8,128)(2,1)S(1)}, bf16[256,512]{1,0:T(8,128)(2,1)}, u32[]{:S(2)}) copy-start(bf16[256,512]{1,0:T(8,128)(2,1)} %pin_ref.1) | copy-start | bytes 786436
  1.3 3.2 %copy-start.2 = (bf16[512,256]{1,0:T(8,128)(2,1)S(1)}, bf16[512,256]{1,0:T(8,128)(2,1)}, u32[]{:S(2)}) copy-start(bf16[512,256]{1,0:T(8,128)(2,1)} %po_ref.1) | copy-start | bytes 786436
  1.3 3.2 %copy-start.3 = (f32[3,512]{1,0:T(4,128)S(1)}, f32[3,512]{1,0:T(4,128)}, u32[]{:S(2)}) copy-start(f32[3,512]{1,0:T(4,128)} %tw_ref.1) | copy-start | bytes 18436
  1.3 3.2 %copy-start.4 = (f32[3,512]{1,0:T(4,128)S(1)}, f32[3,512]{1,0:T(4,128)}, u32[]{:S(2)}) copy-start(f32[3,512]{1,0:T(4,128)} %tt_ref.1) | copy-start | bytes 18436
  1.3 8.6 %copy-start = (f32[256]{0:T(256)S(1)}, f32[256]{0:T(256)}, u32[]{:S(2)}) copy-start(f32[256]{0:T(256)} %param.11) | copy-start | bytes 3076
  1.3 4.2 %collective-permute-start = (bf16[48,256]{1,0:T(8,128)(2,1)S(1)}, bf16[48,256]{1,0:T(8,128)(2,1)S(1)}, u32[]{:S(2)}, u32[]{:S(2)}) collective-permute-start(bf16[48,256]{1,0:T(8,128)(2,1)S(1)} %fusion.2), channel_id=1, source_target_pairs={{0,1},{1,0},{2,3},{3,2},{4,5},{5,4},{6,7},{7,6},{8,9},{9,8},{10,11... | collective-permute-start | bytes 73736 | tf_op jit(solution)/shard_map/ppermute | solution.py:124
  5.6 18.4 %collective-permute-start.2 = (bf16[272,256]{1,0:T(8,128)(2,1)S(1)}, bf16[272,256]{1,0:T(8,128)(2,1)S(1)}, u32[]{:S(2)}, u32[]{:S(2)}) collective-permute-start(bf16[272,256]{1,0:T(8,128)(2,1)S(1)} %get-tuple-element.11), channel_id=1, source_target_pairs={{0,2},{4,6},{8,10},{12,14},{16,18},{20,22},{24,26},{28,30},{2,0},{... | collective-permute-start | bytes 417800 | tf_op jit(solution)/shard_map/ppermute | solution.py:114
  6.7 17.4 %collective-permute-start.1 = (bf16[272,256]{1,0:T(8,128)(2,1)S(1)}, bf16[272,256]{1,0:T(8,128)(2,1)S(1)}, u32[]{:S(2)}, u32[]{:S(2)}) collective-permute-start(bf16[272,256]{1,0:T(8,128)(2,1)S(1)} %get-tuple-element.12), channel_id=1, source_target_pairs={{2,4},{6,8},{10,12},{14,16},{18,20},{22,24},{26,28},{4,2},{8,6},{1... | collective-permute-start | bytes 417800 | tf_op jit(solution)/shard_map/ppermute | solution.py:114

commit v10 on v8

--- a/solution.py
+++ b/solution.py
@@ -19,7 +19,7 @@
     foot = jnp.where(at == 15, tail, right[w - 16 :].astype(F32)).astype(BF16)
     left = jnp.concatenate([head, left[16:]], axis=0)
     right = jnp.concatenate([right[: w - 16], foot], axis=0)
-    return left, x, right
+    return jnp.concatenate([left, x, right], axis=1)
 
 
 def conv_kernel(before, here, after, top, bot, u_ref, lh_ref, rh_ref, bias_ref, out_ref,
@@ -39,12 +39,7 @@
             both(ref[pl.ds(i * n + a, 1), :], ref[pl.ds(i * n + b, 1), :]) for ref in (lh_ref, rh_ref)
         ]
         lhs = with_sides(both(centre(a), centre(b)), lead, tail)
-        c = u_ref.shape[2]
-        parts = [
-            jnp.dot(x, u_ref[k, j * c : (j + 1) * c, :], preferred_element_type=F32)
-            for j, x in enumerate(lhs)
-        ]
-        return parts[0] + parts[1] + parts[2]
+        return jnp.dot(lhs, u_ref[k], preferred_element_type=F32)
 
     def finish(r, half):
         x = here[r].astype(F32)

time: 29.9 us -> 29.4 us (0.983)
  Pallas kernels: 19.9 us -> 19.5 us
    pallas_call x1, Pallas kernels: 16.7 us -> 16.2 us  [on_device(): pl.pallas_call(conv_kernel, grid=(th // n,), out_shape=jax.ShapeDtypeStru...]
where the time goes in v10:
time: 29.4 us; the launch traced here: 29.2 us
  Pallas kernels  19.5 us (66%)
  starting transfers between devices  5.06 us (17%)
  waiting for transfers between devices  4.27 us (15%)
    pallas_call x1, Pallas kernels, on_device(): pl.pallas_call(conv_kernel, grid=(th // n,), out_shape=jax.ShapeDtypeStru...  16.2 us
    ppermute x2, starting transfers between devices, swap(): return lax.ppermute(x, 'row', pairs + [(b, a) for a, b in pairs])  3.76 us
    ppermute x2, waiting for transfers between devices, swap(): return lax.ppermute(x, 'row', pairs + [(b, a) for a, b in pairs])  3.22 us
    ppermute x1, starting transfers between devices, column_halos(): got = lax.ppermute(jnp.where(low, last, first), 'col', [(0, 1), (1, 0)])  1.3 us
    pallas_call x1, Pallas kernels, on_device(): pl.pallas_call(columns_kernel, grid=(1,), out_shape=cols, in_specs=[some_...  1.26 us
    ppermute x1, waiting for transfers between devices, column_halos(): got = lax.ppermute(jnp.where(low, last, first), 'col', [(0, 1), (1, 0)])  1.06 us
    pallas_call x1, Pallas kernels, on_device(): pl.pallas_call(weights_kernel, grid=(1,), out_shape=weights, in_specs=[wh...  1 us
    pallas_call x1, Pallas kernels, on_device(): pl.pallas_call(rows_kernel, grid=(1,), out_shape=rows, in_specs=[one_row(...  0.98 us
  transfers between devices with their start and end apart: 3, of which 2 were waited for; matrix products, arithmetic and copies ran while one was open for 0% of the time, Pallas kernels for 8%

profile of v10, /device:TPU:25, one launch (start us, length us, event | category | flops | bytes accessed | tf_op | source)
XLA Modules:
  0.0 29.2 jit_solution(144689417978174152)
XLA Ops:
  0.0 1.0 %rows.1 = bf16[2,256,256]{2,1,0:T(8,128)(2,1)S(1)} custom-call(bf16[48,256,256]{2,1,0:T(8,128)(2,1)} %after.1, bf16[48,256,256]{2,1,0:T(8,128)(2,1)} %after.1), custom_call_target="tpu_custom_call" | custom-call | tf_op jit(solution)/shard_map/rows/pallas_call | solution.py:130
  1.0 0.7 %collective-permute-start.1 = (bf16[256,256]{1,0:T(8,128)(2,1)S(1)}, bf16[256,256]{1,0:T(8,128)(2,1)S(1)}, u32[]{:S(2)}, u32[]{:S(2)}) collective-permute-start(bf16[256,256]{1,0:T(8,128)(2,1)S(1)} %get-tuple-element.7), channel_id=1, source_target_pairs={{0,2},{4,6},{8,10},{12,14},{16,18},{20,22},{24,26},{28,30},{2,0},{... | collective-permute-start | bytes 393224 | tf_op jit(solution)/shard_map/ppermute | solution.py:99
  1.8 3.0 %collective-permute-start = (bf16[256,256]{1,0:T(8,128)(2,1)S(1)}, bf16[256,256]{1,0:T(8,128)(2,1)S(1)}, u32[]{:S(2)}, u32[]{:S(2)}) collective-permute-start(bf16[256,256]{1,0:T(8,128)(2,1)S(1)} %get-tuple-element.8), channel_id=1, source_target_pairs={{2,4},{6,8},{10,12},{14,16},{18,20},{22,24},{26,28},{4,2},{8,6},{1... | collective-permute-start | bytes 393224 | tf_op jit(solution)/shard_map/ppermute | solution.py:99
  4.8 0.0 copy-start.1
  4.8 0.0 copy-start.2
  4.8 0.0 copy-start.3
  4.8 0.0 copy-start.4
  4.8 0.0 copy-start
  4.8 1.3 %columns.1 = f32[2,48,256]{2,1,0:T(8,128)S(1)} custom-call(bf16[48,256,256]{2,1,0:T(8,128)(2,1)} %after.1, bf16[48,256,256]{2,1,0:T(8,128)(2,1)} %after.1), custom_call_target="tpu_custom_call" | custom-call | bytes 3145728 | tf_op jit(solution)/shard_map/columns/pallas_call | solution.py:142
  6.1 0.1 pad.7.clone
  6.2 0.0 collective-permute-done.1
  6.2 3.2 %collective-permute-done = bf16[256,256]{1,0:T(8,128)(2,1)S(1)} collective-permute-done((bf16[256,256]{1,0:T(8,128)(2,1)S(1)}, bf16[256,256]{1,0:T(8,128)(2,1)S(1)}, u32[]{:S(2)}, u32[]{:S(2)}) %collective-permute-start) | collective-permute-done | bytes 131104 | tf_op jit(solution)/shard_map/ppermute | solution.py:99
  9.5 0.1 maximum_select_fusion
  9.6 1.3 %collective-permute-start.2 = (bf16[64,256]{1,0:T(8,128)(2,1)S(1)}, bf16[64,256]{1,0:T(8,128)(2,1)S(1)}, u32[]{:S(2)}, u32[]{:S(2)}) collective-permute-start(bf16[64,256]{1,0:T(8,128)(2,1)S(1)} %maximum_select_fusion), channel_id=1, source_target_pairs={{0,1},{1,0},{2,3},{3,2},{4,5},{5,4},{6,7},{7,6},{8,9},{9,8},{10,11... | collective-permute-start | bytes 98312 | tf_op jit(solution)/shard_map/ppermute | solution.py:109
  10.9 0.0 copy-done.1
  10.9 0.0 copy-done.2
  10.9 0.0 copy-done.3
  10.9 0.0 copy-done.4
  10.9 1.0 %weights.1.u_ref = bf16[4,768,256]{2,1,0:T(8,128)(2,1)S(1)} custom-call(bf16[256,512]{1,0:T(8,128)(2,1)S(1)} %copy-done.1, f32[3,512]{1,0:T(4,128)S(1)} %copy-done.3, f32[3,512]{1,0:T(4,128)S(1)} %copy-done.4, bf16[512,256]{1,0:T(8,128)(2,1)S(1)} %copy-done.2), custom_call_target="tpu_custom_call" | custom-call | flops 805306368 | bytes 3145728 | tf_op jit(solution)/shard_map/weights/pallas_call | solution.py:155
  11.9 1.1 %collective-permute-done.2 = bf16[64,256]{1,0:T(8,128)(2,1)S(1)} collective-permute-done((bf16[64,256]{1,0:T(8,128)(2,1)S(1)}, bf16[64,256]{1,0:T(8,128)(2,1)S(1)}, u32[]{:S(2)}, u32[]{:S(2)}) %collective-permute-start.2) | collective-permute-done | bytes 32800 | tf_op jit(solution)/shard_map/ppermute | solution.py:109
  13.0 0.0 copy-done
  13.0 16.2 %conv.1 = bf16[48,256,256]{2,1,0:T(8,128)(2,1)} custom-call(bf16[48,256,256]{2,1,0:T(8,128)(2,1)} %after.1, bf16[48,256,256]{2,1,0:T(8,128)(2,1)} %after.1, bf16[48,256,256]{2,1,0:T(8,128)(2,1)} %after.1, bf16[256,256]{1,0:T(8,128)(2,1)S(1)} %get-tuple-element.6.top, bf16[256,256]{1,0:T(8,128)(2,1)S(1)} %get-tuple-element.5.bot, ...), custom_call_target="tpu_custom_call" | custom-call | tf_op jit(solution)/shard_map/conv/pallas_call | solution.py:176
  (7 shorter events, 0.1 us)
Async XLA Ops:
  1.0 5.2 %collective-permute-start.1 = (bf16[256,256]{1,0:T(8,128)(2,1)S(1)}, bf16[256,256]{1,0:T(8,128)(2,1)S(1)}, u32[]{:S(2)}, u32[]{:S(2)}) collective-permute-start(bf16[256,256]{1,0:T(8,128)(2,1)S(1)} %get-tuple-element.7), channel_id=1, source_target_pairs={{0,2},{4,6},{8,10},{12,14},{16,18},{20,22},{24,26},{28,30},{2,0},{... | collective-permute-start | bytes 393224 | tf_op jit(solution)/shard_map/ppermute | solution.py:99
  1.8 7.7 %collective-permute-start = (bf16[256,256]{1,0:T(8,128)(2,1)S(1)}, bf16[256,256]{1,0:T(8,128)(2,1)S(1)}, u32[]{:S(2)}, u32[]{:S(2)}) collective-permute-start(bf16[256,256]{1,0:T(8,128)(2,1)S(1)} %get-tuple-element.8), channel_id=1, source_target_pairs={{2,4},{6,8},{10,12},{14,16},{18,20},{22,24},{26,28},{4,2},{8,6},{1... | collective-permute-start | bytes 393224 | tf_op jit(solution)/shard_map/ppermute | solution.py:99
  4.8 6.1 %copy-start.1 = (bf16[256,512]{1,0:T(8,128)(2,1)S(1)}, bf16[256,512]{1,0:T(8,128)(2,1)}, u32[]{:S(2)}) copy-start(bf16[256,512]{1,0:T(8,128)(2,1)} %pin_ref.1) | copy-start | bytes 786436
  4.8 6.1 %copy-start.2 = (bf16[512,256]{1,0:T(8,128)(2,1)S(1)}, bf16[512,256]{1,0:T(8,128)(2,1)}, u32[]{:S(2)}) copy-start(bf16[512,256]{1,0:T(8,128)(2,1)} %po_ref.1) | copy-start | bytes 786436
  4.8 6.1 %copy-start.3 = (f32[3,512]{1,0:T(4,128)S(1)}, f32[3,512]{1,0:T(4,128)}, u32[]{:S(2)}) copy-start(f32[3,512]{1,0:T(4,128)} %tw_ref.1) | copy-start | bytes 18436
  4.8 6.1 %copy-start.4 = (f32[3,512]{1,0:T(4,128)S(1)}, f32[3,512]{1,0:T(4,128)}, u32[]{:S(2)}) copy-start(f32[3,512]{1,0:T(4,128)} %tt_ref.1) | copy-start | bytes 18436
  4.8 8.1 %copy-start = (f32[256]{0:T(256)S(1)}, f32[256]{0:T(256)}, u32[]{:S(2)}) copy-start(f32[256]{0:T(256)} %param.11) | copy-start | bytes 3076
  9.6 3.4 %collective-permute-start.2 = (bf16[64,256]{1,0:T(8,128)(2,1)S(1)}, bf16[64,256]{1,0:T(8,128)(2,1)S(1)}, u32[]{:S(2)}, u32[]{:S(2)}) collective-permute-start(bf16[64,256]{1,0:T(8,128)(2,1)S(1)} %maximum_select_fusion), channel_id=1, source_target_pairs={{0,1},{1,0},{2,3},{3,2},{4,5},{5,4},{6,7},{7,6},{8,9},{9,8},{10,11... | collective-permute-start | bytes 98312 | tf_op jit(solution)/shard_map/ppermute | solution.py:109

commit v11 on v10

--- a/solution.py
+++ b/solution.py
@@ -8,7 +8,7 @@
 BF16 = jnp.bfloat16
 F32 = jnp.float32
 MIB = 1 << 20
-ROWS = 8
+ROWS = 12
 
 
 def with_sides(x, lead, tail):
@@ -48,12 +48,12 @@
     ends[0] = jnp.where(i == 0, top[...], before[0])
     ends[1] = jnp.where(i == pl.num_programs(0) - 1, bot[...], after[0])
     for r in range(0, n, 2):
-        m1 = product(1, r + 1, r + 2, True)
+        m1 = product(1, r + 1, r + 2, True) + bias
         m2 = product(2, r + 2, r + 1, False)
         m0 = product(0, r, r + 2, False)
         m3 = product(3, r + 1, r + 3, False)
-        finish(r, m0 + (m1 + m2) + bias)
-        finish(r + 1, (m1 - m2) - m3 + bias)
+        finish(r, m0 + (m1 + m2))
+        finish(r + 1, (m1 - m2) - m3)
 
 
 def rows_kernel(first, last, rows_ref):

time: 29.4 us -> 29.3 us (level)
  no operation moved by 1% of the time
where the time goes in v11:
time: 29.3 us; the launch traced here: 29.1 us
  Pallas kernels  19.4 us (66%)
  starting transfers between devices  5.06 us (17%)
  waiting for transfers between devices  4.27 us (15%)
    pallas_call x1, Pallas kernels, on_device(): pl.pallas_call(conv_kernel, grid=(th // n,), out_shape=jax.ShapeDtypeStru...  16.2 us
    ppermute x2, starting transfers between devices, swap(): return lax.ppermute(x, 'row', pairs + [(b, a) for a, b in pairs])  3.76 us
    ppermute x2, waiting for transfers between devices, swap(): return lax.ppermute(x, 'row', pairs + [(b, a) for a, b in pairs])  3.22 us
    ppermute x1, starting transfers between devices, column_halos(): got = lax.ppermute(jnp.where(low, last, first), 'col', [(0, 1), (1, 0)])  1.3 us
    pallas_call x1, Pallas kernels, on_device(): pl.pallas_call(columns_kernel, grid=(1,), out_shape=cols, in_specs=[some_...  1.26 us
    ppermute x1, waiting for transfers between devices, column_halos(): got = lax.ppermute(jnp.where(low, last, first), 'col', [(0, 1), (1, 0)])  1.06 us
    pallas_call x1, Pallas kernels, on_device(): pl.pallas_call(weights_kernel, grid=(1,), out_shape=weights, in_specs=[wh...  1 us
    pallas_call x1, Pallas kernels, on_device(): pl.pallas_call(rows_kernel, grid=(1,), out_shape=rows, in_specs=[one_row(...  0.98 us
  transfers between devices with their start and end apart: 3, of which 2 were waited for; matrix products, arithmetic and copies ran while one was open for 0% of the time, Pallas kernels for 8%

profile of v11, /device:TPU:25, one launch (start us, length us, event | category | flops | bytes accessed | tf_op | source)
XLA Modules:
  0.0 29.1 jit_solution(4607281343761935745)
XLA Ops:
  0.0 1.0 %rows.1 = bf16[2,256,256]{2,1,0:T(8,128)(2,1)S(1)} custom-call(bf16[48,256,256]{2,1,0:T(8,128)(2,1)} %after.1, bf16[48,256,256]{2,1,0:T(8,128)(2,1)} %after.1), custom_call_target="tpu_custom_call" | custom-call | tf_op jit(solution)/shard_map/rows/pallas_call | solution.py:130
  1.0 0.7 %collective-permute-start.1 = (bf16[256,256]{1,0:T(8,128)(2,1)S(1)}, bf16[256,256]{1,0:T(8,128)(2,1)S(1)}, u32[]{:S(2)}, u32[]{:S(2)}) collective-permute-start(bf16[256,256]{1,0:T(8,128)(2,1)S(1)} %get-tuple-element.7), channel_id=1, source_target_pairs={{0,2},{4,6},{8,10},{12,14},{16,18},{20,22},{24,26},{28,30},{2,0},{... | collective-permute-start | bytes 393224 | tf_op jit(solution)/shard_map/ppermute | solution.py:99
  1.8 3.0 %collective-permute-start = (bf16[256,256]{1,0:T(8,128)(2,1)S(1)}, bf16[256,256]{1,0:T(8,128)(2,1)S(1)}, u32[]{:S(2)}, u32[]{:S(2)}) collective-permute-start(bf16[256,256]{1,0:T(8,128)(2,1)S(1)} %get-tuple-element.8), channel_id=1, source_target_pairs={{2,4},{6,8},{10,12},{14,16},{18,20},{22,24},{26,28},{4,2},{8,6},{1... | collective-permute-start | bytes 393224 | tf_op jit(solution)/shard_map/ppermute | solution.py:99
  4.8 0.0 copy-start.1
  4.8 0.0 copy-start.2
  4.8 0.0 copy-start.3
  4.8 0.0 copy-start.4
  4.8 0.0 copy-start
  4.8 1.3 %columns.1 = f32[2,48,256]{2,1,0:T(8,128)S(1)} custom-call(bf16[48,256,256]{2,1,0:T(8,128)(2,1)} %after.1, bf16[48,256,256]{2,1,0:T(8,128)(2,1)} %after.1), custom_call_target="tpu_custom_call" | custom-call | bytes 3145728 | tf_op jit(solution)/shard_map/columns/pallas_call | solution.py:142
  6.1 0.1 pad.7.clone
  6.2 0.0 collective-permute-done.1
  6.2 3.2 %collective-permute-done = bf16[256,256]{1,0:T(8,128)(2,1)S(1)} collective-permute-done((bf16[256,256]{1,0:T(8,128)(2,1)S(1)}, bf16[256,256]{1,0:T(8,128)(2,1)S(1)}, u32[]{:S(2)}, u32[]{:S(2)}) %collective-permute-start) | collective-permute-done | bytes 131104 | tf_op jit(solution)/shard_map/ppermute | solution.py:99
  9.5 0.1 maximum_select_fusion
  9.6 1.3 %collective-permute-start.2 = (bf16[64,256]{1,0:T(8,128)(2,1)S(1)}, bf16[64,256]{1,0:T(8,128)(2,1)S(1)}, u32[]{:S(2)}, u32[]{:S(2)}) collective-permute-start(bf16[64,256]{1,0:T(8,128)(2,1)S(1)} %maximum_select_fusion), channel_id=1, source_target_pairs={{0,1},{1,0},{2,3},{3,2},{4,5},{5,4},{6,7},{7,6},{8,9},{9,8},{10,11... | collective-permute-start | bytes 98312 | tf_op jit(solution)/shard_map/ppermute | solution.py:109
  10.9 0.0 copy-done.1
  10.9 0.0 copy-done.2
  10.9 0.0 copy-done.3
  10.9 0.0 copy-done.4
  10.9 1.0 %weights.1.u_ref = bf16[4,768,256]{2,1,0:T(8,128)(2,1)S(1)} custom-call(bf16[256,512]{1,0:T(8,128)(2,1)S(1)} %copy-done.1, f32[3,512]{1,0:T(4,128)S(1)} %copy-done.3, f32[3,512]{1,0:T(4,128)S(1)} %copy-done.4, bf16[512,256]{1,0:T(8,128)(2,1)S(1)} %copy-done.2), custom_call_target="tpu_custom_call" | custom-call | flops 805306368 | bytes 3145728 | tf_op jit(solution)/shard_map/weights/pallas_call | solution.py:155
  11.9 1.1 %collective-permute-done.2 = bf16[64,256]{1,0:T(8,128)(2,1)S(1)} collective-permute-done((bf16[64,256]{1,0:T(8,128)(2,1)S(1)}, bf16[64,256]{1,0:T(8,128)(2,1)S(1)}, u32[]{:S(2)}, u32[]{:S(2)}) %collective-permute-start.2) | collective-permute-done | bytes 32800 | tf_op jit(solution)/shard_map/ppermute | solution.py:109
  13.0 0.0 copy-done
  13.0 16.2 %conv.1 = bf16[48,256,256]{2,1,0:T(8,128)(2,1)} custom-call(bf16[48,256,256]{2,1,0:T(8,128)(2,1)} %after.1, bf16[48,256,256]{2,1,0:T(8,128)(2,1)} %after.1, bf16[48,256,256]{2,1,0:T(8,128)(2,1)} %after.1, bf16[256,256]{1,0:T(8,128)(2,1)S(1)} %get-tuple-element.6.top, bf16[256,256]{1,0:T(8,128)(2,1)S(1)} %get-tuple-element.5.bot, ...), custom_call_target="tpu_custom_call" | custom-call | tf_op jit(solution)/shard_map/conv/pallas_call | solution.py:176
  (7 shorter events, 0.1 us)
Async XLA Ops:
  1.0 5.2 %collective-permute-start.1 = (bf16[256,256]{1,0:T(8,128)(2,1)S(1)}, bf16[256,256]{1,0:T(8,128)(2,1)S(1)}, u32[]{:S(2)}, u32[]{:S(2)}) collective-permute-start(bf16[256,256]{1,0:T(8,128)(2,1)S(1)} %get-tuple-element.7), channel_id=1, source_target_pairs={{0,2},{4,6},{8,10},{12,14},{16,18},{20,22},{24,26},{28,30},{2,0},{... | collective-permute-start | bytes 393224 | tf_op jit(solution)/shard_map/ppermute | solution.py:99
  1.8 7.7 %collective-permute-start = (bf16[256,256]{1,0:T(8,128)(2,1)S(1)}, bf16[256,256]{1,0:T(8,128)(2,1)S(1)}, u32[]{:S(2)}, u32[]{:S(2)}) collective-permute-start(bf16[256,256]{1,0:T(8,128)(2,1)S(1)} %get-tuple-element.8), channel_id=1, source_target_pairs={{2,4},{6,8},{10,12},{14,16},{18,20},{22,24},{26,28},{4,2},{8,6},{1... | collective-permute-start | bytes 393224 | tf_op jit(solution)/shard_map/ppermute | solution.py:99
  4.8 6.1 %copy-start.1 = (bf16[256,512]{1,0:T(8,128)(2,1)S(1)}, bf16[256,512]{1,0:T(8,128)(2,1)}, u32[]{:S(2)}) copy-start(bf16[256,512]{1,0:T(8,128)(2,1)} %pin_ref.1) | copy-start | bytes 786436
  4.8 6.1 %copy-start.2 = (bf16[512,256]{1,0:T(8,128)(2,1)S(1)}, bf16[512,256]{1,0:T(8,128)(2,1)}, u32[]{:S(2)}) copy-start(bf16[512,256]{1,0:T(8,128)(2,1)} %po_ref.1) | copy-start | bytes 786436
  4.8 6.1 %copy-start.3 = (f32[3,512]{1,0:T(4,128)S(1)}, f32[3,512]{1,0:T(4,128)}, u32[]{:S(2)}) copy-start(f32[3,512]{1,0:T(4,128)} %tw_ref.1) | copy-start | bytes 18436
  4.8 6.1 %copy-start.4 = (f32[3,512]{1,0:T(4,128)S(1)}, f32[3,512]{1,0:T(4,128)}, u32[]{:S(2)}) copy-start(f32[3,512]{1,0:T(4,128)} %tt_ref.1) | copy-start | bytes 18436
  4.8 8.1 %copy-start = (f32[256]{0:T(256)S(1)}, f32[256]{0:T(256)}, u32[]{:S(2)}) copy-start(f32[256]{0:T(256)} %param.11) | copy-start | bytes 3076
  9.6 3.4 %collective-permute-start.2 = (bf16[64,256]{1,0:T(8,128)(2,1)S(1)}, bf16[64,256]{1,0:T(8,128)(2,1)S(1)}, u32[]{:S(2)}, u32[]{:S(2)}) collective-permute-start(bf16[64,256]{1,0:T(8,128)(2,1)S(1)} %maximum_select_fusion), channel_id=1, source_target_pairs={{0,1},{1,0},{2,3},{3,2},{4,5},{5,4},{6,7},{7,6},{8,9},{9,8},{10,11... | collective-permute-start | bytes 98312 | tf_op jit(solution)/shard_map/ppermute | solution.py:109
